TPU v7x, 128 devices: a whole 4x4x4 slice. The times are simulated.
128 devices in a mesh: front: 4 (over x), helper: 32 (over z, y, core).
Axes of the slice: x: 4, y: 4, z: 4, core: 2. Of those that a mesh axis runs over, the one named last changes fastest.
Arguments:
- front: float32 [4, 8192, 8192], P('front', 'helper'), as said below
- tile_map: int32 [4, 52], P('front'), may hold values from 0 to 63, as said below
- live_tiles: int32 [4], P('front'), may hold values from 26 to 52, as said below
Outputs:
- factor: float32 [4, 8192, 1536], P('front', 'helper')
- pivots: float32 [4, 1536], P('front')
- parent: bfloat16 [4, 8192, 8192], P('front', 'helper')
Inputs may be any that keep to these rules, and one draw needn't show every extreme that they name: `tile_map`: the 52 entries of one front are distinct. `live_tiles`: some front has all 52 tiles live. Each front is symmetric and positive definite.
All inputs are finite; a program needn't handle non-finite values.
Results may differ from a plain program's by a relative error of at most 0.0021.
Values may be sent and summed in bfloat16 or wider, within the bound.
No kernel may reach another device: no remote copies, remote signals or barrier semaphores. Data moves between devices by JAX's collectives and lax.ppermute only.
A program may use at most 192 MiB of HBM per device.

v0:
```python
import jax
import jax.numpy as jnp
from jax import lax
from jax.sharding import PartitionSpec as P

PB = 512
NPB = 3
TILE = 128
NPIV = 1536
CT = 52
PT = 64


def shifted(array, axis, by):
    count = lax.axis_size(axis)
    return lax.ppermute(array, axis, [(i, (i + by) % count) for i in range(count)])


def rows_in_range(values, first_row, lower_bound, count):
    offsets = lax.iota(jnp.int32, count) + lower_bound - first_row
    inside = (offsets >= 0) & (offsets < values.shape[0])
    picked = jnp.take(values, jnp.clip(offsets, 0, values.shape[0] - 1), axis=0)
    return jnp.where(inside[:, None], picked, jnp.float32(0.0))


def local(front, tile_map, live_tiles):
    matrix = front[0]
    row_count, ordering_length = matrix.shape
    helpers = lax.axis_size("helper")
    first_row = lax.axis_index("helper") * row_count
    global_rows = first_row + lax.iota(jnp.int32, row_count)
    column_ids = lax.iota(jnp.int32, ordering_length)
    columns = []
    pivot_list = []
    for block_index in range(NPB):
        lower_bound = block_index * PB
        high_edge = lower_bound + PB
        pivot_block = lax.psum(
            rows_in_range(matrix[:, lower_bound:high_edge], first_row, lower_bound, PB), "helper"
        )
        chol_block = jnp.linalg.cholesky(pivot_block)
        panel = matrix[:, lower_bound:high_edge]
        scaled = jax.scipy.linalg.solve_triangular(chol_block, panel.T, lower=True).T
        scaled = jnp.where((global_rows >= lower_bound)[:, None], scaled, jnp.float32(0.0))
        diag_values = jnp.diagonal(chol_block)
        columns.append(scaled / diag_values[None, :])
        pivot_list.append(diag_values * diag_values)
        rounded = scaled.astype(jnp.bfloat16)
        schur_update = lax.dot_general(
            rounded,
            lax.all_gather(rounded, "helper", axis=0, tiled=True),
            (((1,), (1,)), ((), ())),
            preferred_element_type=jnp.float32,
        )
        matrix = matrix - jnp.where(
            (column_ids >= high_edge)[None, :], schur_update, jnp.float32(0.0)
        )
    factor_cols = jnp.concatenate(columns, axis=1)
    pivot_values = jnp.concatenate(pivot_list)
    live_count = live_tiles[0]
    mapping = tile_map[0]
    row_tiles = (global_rows - NPIV) // TILE
    row_live = (global_rows >= NPIV) & (row_tiles < live_count)
    contrib = jnp.where(row_live[:, None], matrix[:, NPIV:], jnp.float32(0.0)).astype(jnp.bfloat16)
    picker_matrix = (
        (mapping[None, :] == lax.iota(jnp.int32, PT)[:, None])
        & (lax.iota(jnp.int32, CT)[None, :] < live_count)
    ).astype(jnp.bfloat16)
    outgoing = jnp.einsum(
        "ruc,Iu->rIc",
        contrib.reshape(row_count, CT, TILE),
        picker_matrix,
        preferred_element_type=jnp.float32,
    )
    outgoing = outgoing.astype(jnp.bfloat16).reshape(row_count, helpers, row_count)
    incoming = lax.all_to_all(outgoing, "helper", split_axis=1, concat_axis=0, tiled=True)
    offspring_rows = incoming.reshape(ordering_length, row_count)[NPIV:].reshape(
        CT, TILE, row_count
    )
    positioned = jnp.einsum(
        "rj,jkp->rkp", picker_matrix, offspring_rows, preferred_element_type=jnp.float32
    )
    parent_rows = positioned.reshape(ordering_length, row_count).T.astype(jnp.bfloat16)
    parent_rows = shifted(parent_rows, "front", 1)
    return (factor_cols[None], pivot_values[None], parent_rows[None])


def solution(mesh):
    placed = (P("front", "helper", None), P("front", None), P("front"))
    return jax.shard_map(
        local,
        mesh=mesh,
        in_specs=placed,
        out_specs=(P("front", "helper", None), P("front", None), P("front", "helper", None)),
        check_vma=False,
    )
```

profile of v0, /device:TPU:0, one launch (start us, length us, event | category | flops | bytes accessed | tf_op | source)
XLA Modules:
  0.0 1174.6 jit_solution(9802192539638831089)
XLA Ops:
  8.4 1.6 gather_fusion.3
  11.6 107.8 %all-reduce.5.cloned.1.call-done = f32[512,512]{0,1:T(8,128)} async-done(((f32[512,512]{0,1:T(8,128)}), f32[512,512]{0,1:T(8,128)}) %all-reduce.5.cloned.1.call-update) | async-done | bytes 1048592 | tf_op jit(solution)/shard_map/psum | solution.py:38
  119.4 1.6 copy.14
  121.0 1.4 fusion.11
  122.4 11.7 cholesky.374
  134.8 9.8 custom-call.37
  145.4 11.7 cholesky.393
  157.9 18.5 %custom-call.38 = f32[1,128,128]{1,2,0:T(8,128)S(1)} custom-call(f32[1,128,128]{2,1,0:T(8,128)S(1)} %get-tuple-element.103), custom_call_target="InvertDiagBlocksLowerTriangular" | custom-call | tf_op jit(solution)/shard_map/jit(cholesky)/cholesky | solution.py:41
  177.1 11.7 cholesky.414
  189.5 9.8 custom-call.39
  199.9 11.7 cholesky.431
  216.3 8.1 while.6
  224.5 39.3 %custom-call.40 = f32[4,128,128]{1,2,0:T(8,128)S(1)} custom-call(f32[4,128,128]{2,1,0:T(8,128)S(1)} %get-tuple-element.26), custom_call_target="InvertDiagBlocksLowerTriangular" | custom-call | tf_op jit(solution)/shard_map/jit(_solve_triangular)/triangular_solve | solution.py:43
  267.8 59.3 %all-gather.4.cloned.1.call-done = bf16[8192,512]{0,1:T(8,128)(2,1)} async-done(((bf16[256,512]{0,1:T(8,128)(2,1)}), bf16[8192,512]{0,1:T(8,128)(2,1)}) %all-gather.4.cloned.1.call-update) | async-done | bytes 8388624 | tf_op jit(solution)/shard_map/all_gather | solution.py:51
  327.1 8.3 fusion
  335.5 3.2 copy-done
  338.8 1.6 gather_fusion.4
  342.4 104.4 %all-reduce.7.cloned.1.call-done = f32[512,512]{0,1:T(8,128)} async-done(((f32[512,512]{0,1:T(8,128)}), f32[512,512]{0,1:T(8,128)}) %all-reduce.7.cloned.1.call-update) | async-done | bytes 1048592 | tf_op jit(solution)/shard_map/psum | solution.py:38
  446.8 1.6 copy.16
  449.8 11.7 cholesky.446
  462.2 9.8 custom-call.41
  472.8 11.7 cholesky.465
  485.3 10.0 custom-call.42
  495.9 11.7 cholesky.486
  508.4 9.8 custom-call.43
  518.8 11.7 cholesky.503
  533.8 1.5 fusion.13
  535.3 8.5 while.7
  543.7 39.3 %custom-call.44 = f32[4,128,128]{1,2,0:T(8,128)S(1)} custom-call(f32[4,128,128]{2,1,0:T(8,128)S(1)} %get-tuple-element.27), custom_call_target="InvertDiagBlocksLowerTriangular" | custom-call | tf_op jit(solution)/shard_map/jit(_solve_triangular)/triangular_solve | solution.py:43
  587.1 59.3 %all-gather.6.cloned.1.call-done = bf16[8192,512]{0,1:T(8,128)(2,1)} async-done(((bf16[256,512]{0,1:T(8,128)(2,1)}), bf16[8192,512]{0,1:T(8,128)(2,1)}) %all-gather.6.cloned.1.call-update) | async-done | bytes 8388624 | tf_op jit(solution)/shard_map/all_gather | solution.py:51
  646.4 8.4 fusion.1
  654.7 3.2 copy-done.1
  658.1 1.6 gather_fusion.5
  661.6 104.4 %all-reduce.9.cloned.1.call-done = f32[512,512]{0,1:T(8,128)} async-done(((f32[512,512]{0,1:T(8,128)}), f32[512,512]{0,1:T(8,128)}) %all-reduce.9.cloned.1.call-update) | async-done | bytes 1048592 | tf_op jit(solution)/shard_map/psum | solution.py:38
  766.0 1.6 copy.18
  769.1 11.7 cholesky.518
  781.5 9.8 custom-call.45
  792.1 11.7 cholesky.537
  804.5 10.0 custom-call.46
  815.1 11.7 cholesky.558
  827.6 9.8 custom-call.47
  838.0 11.7 cholesky.575
  853.0 1.5 fusion.12
  854.5 7.7 while.8
  862.2 39.3 %custom-call.48 = f32[4,128,128]{1,2,0:T(8,128)S(1)} custom-call(f32[4,128,128]{2,1,0:T(8,128)S(1)} %get-tuple-element.28), custom_call_target="InvertDiagBlocksLowerTriangular" | custom-call | tf_op jit(solution)/shard_map/jit(_solve_triangular)/triangular_solve | solution.py:43
  906.7 58.1 %all-gather.8.cloned.1.call-done = bf16[8192,512]{0,1:T(8,128)(2,1)} async-done(((bf16[256,512]{0,1:T(8,128)(2,1)}), bf16[8192,512]{0,1:T(8,128)(2,1)}) %all-gather.8.cloned.1.call-update) | async-done | bytes 8388624 | tf_op jit(solution)/shard_map/all_gather | solution.py:51
  964.8 5.9 fusion.130
  970.7 4.9 fusion.3
  975.6 4.8 copy.19
  980.4 4.9 copy.20
  985.3 5.4 convert_bitcast_fusion
  990.7 7.3 reshape.133
  998.1 4.6 copy.21
  1002.6 56.4 %all_to_all.15 = bf16[256,32,256]{2,0,1:T(8,128)(2,1)S(1)} all-to-all(bf16[256,32,256]{2,0,1:T(8,128)(2,1)S(1)} %copy.21), channel_id=1, replica_groups=mesh['front'=4,'helper'=32] {'helper'}, dimensions={1} | all-to-all | bytes 8388608 | tf_op jit(solution)/shard_map/all_to_all | solution.py:76
  1059.3 3.1 fusion.6
  1062.5 4.4 copy.23
  1066.9 1.5 collective-permute-start
  1068.4 4.5 gather_fusion
  1072.9 2.0 divide_bitcast_fusion.2
  1074.9 4.5 gather_fusion.1
  1080.6 4.5 gather_fusion.2
  1088.2 1.6 copy.24
  1089.8 71.2 %collective-permute-done = bf16[256,8192]{0,1:T(8,128)(2,1)} collective-permute-done((bf16[256,8192]{0,1:T(8,128)(2,1)}, bf16[256,8192]{0,1:T(8,128)(2,1)}, u32[]{:S(2)}, u32[]{:S(2)}) %collective-permute-start) | collective-permute-done | bytes 4194336 | tf_op jit(solution)/shard_map/ppermute | solution.py:16
  1161.0 6.3 copy.25
  (207 shorter events, 66.4 us)
Async XLA Ops:
  7.2 112.2 %all-reduce.5.cloned.1.call-start = ((), (), s32[]{:S(2)}) async-start(), calls=%async_computation.1 | async-start | bytes 2097152 | tf_op jit(solution)/shard_map/psum | solution.py:38
  11.5 315.6 %all-gather.4.cloned.1.call-start = ((), (), s32[]{:S(2)}) async-start(), calls=%async_computation.2 | async-start | bytes 8650752 | tf_op jit(solution)/shard_map/all_gather | solution.py:51
  264.9 62.3 %copy-start.8 = (f32[128,256]{1,0:T(8,128)}, f32[128,256]{1,0:T(8,128)S(1)}, u32[]{:S(2)}) copy-start(f32[128,256]{1,0:T(8,128)S(1)} %fusion.88) | copy-start | bytes 393220
  265.8 61.3 %copy-start.11 = (f32[128,256]{1,0:T(8,128)}, f32[128,256]{1,0:T(8,128)S(1)}, u32[]{:S(2)}) copy-start(f32[128,256]{1,0:T(8,128)S(1)} %fusion.86) | copy-start | bytes 393220
  266.9 60.2 %copy-start.14 = (f32[128,256]{1,0:T(8,128)}, f32[128,256]{1,0:T(8,128)S(1)}, u32[]{:S(2)}) copy-start(f32[128,256]{1,0:T(8,128)S(1)} %fusion.85) | copy-start | bytes 393220
  267.7 179.1 %all-reduce.7.cloned.1.call-start = ((), (), s32[]{:S(2)}) async-start(), calls=%async_computation.3 | async-start | bytes 2097152 | tf_op jit(solution)/shard_map/psum | solution.py:38
  335.5 3.2 copy-start
  341.9 304.4 %all-gather.6.cloned.1.call-start = ((), (), s32[]{:S(2)}) async-start(), calls=%async_computation.4 | async-start | bytes 8650752 | tf_op jit(solution)/shard_map/all_gather | solution.py:51
  583.4 63.0 %copy-start.5 = (f32[128,256]{1,0:T(8,128)}, f32[128,256]{1,0:T(8,128)S(1)}, u32[]{:S(2)}) copy-start(f32[128,256]{1,0:T(8,128)S(1)} %fusion.64) | copy-start | bytes 393220
  584.1 62.3 %copy-start.9 = (f32[128,256]{1,0:T(8,128)}, f32[128,256]{1,0:T(8,128)S(1)}, u32[]{:S(2)}) copy-start(f32[128,256]{1,0:T(8,128)S(1)} %fusion.82) | copy-start | bytes 393220
  585.0 61.3 %copy-start.12 = (f32[128,256]{1,0:T(8,128)}, f32[128,256]{1,0:T(8,128)S(1)}, u32[]{:S(2)}) copy-start(f32[128,256]{1,0:T(8,128)S(1)} %fusion.80) | copy-start | bytes 393220
  586.2 60.2 %copy-start.15 = (f32[128,256]{1,0:T(8,128)}, f32[128,256]{1,0:T(8,128)S(1)}, u32[]{:S(2)}) copy-start(f32[128,256]{1,0:T(8,128)S(1)} %fusion.79) | copy-start | bytes 393220
  587.0 179.1 %all-reduce.9.cloned.1.call-start = ((), (), s32[]{:S(2)}) async-start(), calls=%async_computation.5 | async-start | bytes 2097152 | tf_op jit(solution)/shard_map/psum | solution.py:38
  654.7 3.2 copy-start.1
  661.2 303.6 %all-gather.8.cloned.1.call-start = ((), (), s32[]{:S(2)}) async-start(), calls=%async_computation.6 | async-start | bytes 8650752 | tf_op jit(solution)/shard_map/all_gather | solution.py:51
  901.8 68.9 %copy-start.7 = (f32[128,256]{1,0:T(8,128)}, f32[128,256]{1,0:T(8,128)S(1)}, u32[]{:S(2)}) copy-start(f32[128,256]{1,0:T(8,128)S(1)} %fusion.59) | copy-start | bytes 393220
  902.5 68.2 %copy-start.10 = (f32[128,256]{1,0:T(8,128)}, f32[128,256]{1,0:T(8,128)S(1)}, u32[]{:S(2)}) copy-start(f32[128,256]{1,0:T(8,128)S(1)} %fusion.76) | copy-start | bytes 393220
  903.5 67.2 %copy-start.13 = (f32[128,256]{1,0:T(8,128)}, f32[128,256]{1,0:T(8,128)S(1)}, u32[]{:S(2)}) copy-start(f32[128,256]{1,0:T(8,128)S(1)} %fusion.74) | copy-start | bytes 393220
  904.6 66.1 %copy-start.16 = (f32[128,256]{1,0:T(8,128)}, f32[128,256]{1,0:T(8,128)S(1)}, u32[]{:S(2)}) copy-start(f32[128,256]{1,0:T(8,128)S(1)} %fusion.73) | copy-start | bytes 393220
  975.6 9.7 copy-start.17
  1002.6 56.7 %copy-start.18 = (pred[52]{0:T(512)(128)(4,1)S(1)}, pred[52]{0:T(512)(128)(4,1)}, u32[]{:S(2)}) copy-start(pred[52]{0:T(512)(128)(4,1)} %iota_compare_fusion.7) | copy-start | bytes 160
  1059.3 9.0 copy-start.2
  1062.4 12.5 %copy-start.3 = (f32[512,512]{1,0:T(8,128)S(1)}, f32[512,512]{1,0:T(8,128)}, u32[]{:S(2)}) copy-start(f32[512,512]{1,0:T(8,128)} %get-tuple-element.62) | copy-start | bytes 3145732
  1062.4 17.0 %copy-start.6 = (f32[128,256]{1,0:T(8,128)S(1)}, f32[128,256]{1,0:T(8,128)}, u32[]{:S(2)}) copy-start(f32[128,256]{1,0:T(8,128)} %copy-done.5) | copy-start | bytes 393220
  1062.4 18.2 %copy-start.4 = (f32[512,512]{1,0:T(8,128)S(1)}, f32[512,512]{1,0:T(8,128)}, u32[]{:S(2)}) copy-start(f32[512,512]{1,0:T(8,128)} %get-tuple-element.60) | copy-start | bytes 3145732
  1066.9 94.1 %collective-permute-start = (bf16[256,8192]{0,1:T(8,128)(2,1)}, bf16[256,8192]{0,1:T(8,128)(2,1)}, u32[]{:S(2)}, u32[]{:S(2)}) collective-permute-start(bf16[256,8192]{0,1:T(8,128)(2,1)} %bitcast.54), channel_id=1, source_target_pairs={{0,32},{32,64},{64,96},{96,0},{1,33},{33,65},{65,97},{97,1},{2,34}... | collective-permute-start | bytes 12582920 | tf_op jit(solution)/shard_map/ppermute | solution.py:16
Sparse Core Ops, SparseCore 0:
  11.8 107.5 all-reduce.4
  267.8 59.2 all-gather.3
  342.0 104.6 all-reduce.6
  587.1 59.2 all-gather.5
  661.3 104.7 all-reduce.8
  905.5 59.2 all-gather.7
where the time goes:
time: 1190 us; the launch traced here: 1170 us
  waiting for transfers between devices  565 us (47%)
  other arithmetic  390 us (33%)
  local copies, waits for them, and re-layouts  91.2 us (8%)
  blocking collectives  56.4 us (5%)
  matrix products  45.9 us (4%)
  between operations  23.9 us (2%)
    psum x3, waiting for transfers between devices, local(): lax.psum(rows_in_range(matrix[:, lower_bound:high_edge], first_row, lower...  317 us
    another operation x45, other arithmetic, local(): chol_block = jnp.linalg.cholesky(pivot_block)  246 us
    all_gather x3, waiting for transfers between devices, local(): lax.all_gather(rounded, 'helper', axis=0, tiled=True)  177 us
    another operation x7, other arithmetic, local(): jax.scipy.linalg.solve_triangular(chol_block, panel.T, lower=True)  122 us
    ppermute x1, waiting for transfers between devices, shifted(): lax.ppermute(array, axis, [(i, (i + by) % count) for i in range(count)])  71.2 us
    all_to_all x1, blocking collectives, local(): lax.all_to_all(outgoing, 'helper', split_axis=1, concat_axis=0, tiled=True)  56.4 us
    another operation x40, local copies, waits for them, and re-layouts, local(): jax.scipy.linalg.solve_triangular(chol_block, panel.T, lower=True)  24.1 us
  transfers between devices with their start and end apart: 7, of which 7 were waited for; matrix products, arithmetic and copies ran while one was open for 2% of the time, Pallas kernels for 0%

commit v1 on v0

v1 whole, which is shorter than its diff:
```python
import functools

import jax
import jax.numpy as jnp
from jax import lax
from jax.experimental import pallas as pl
from jax.experimental.pallas import tpu as pltpu
from jax.sharding import PartitionSpec as P

PB = 512
NPB = 3
TILE = 128
NPIV = 1536
CT = 52
PT = 64
SKIP = NPIV // TILE
VMEM_LIMIT = 48 << 20
HIGHEST = lax.Precision.HIGHEST


def shifted(array, axis, by):
    count = lax.axis_size(axis)
    return lax.ppermute(array, axis, [(i, (i + by) % count) for i in range(count)])


def dot_nt(a, b, precision=None):
    return lax.dot_general(
        a, b, (((1,), (1,)), ((), ())), precision=precision, preferred_element_type=jnp.float32
    )


def dot_nn(a, b, precision=None):
    return lax.dot_general(
        a, b, (((1,), (0,)), ((), ())), precision=precision, preferred_element_type=jnp.float32
    )


def leaf_inverse(strips):
    lanes = lax.broadcasted_iota(jnp.int32, (8, TILE), 1)
    subs = lax.broadcasted_iota(jnp.int32, (8, TILE), 0)
    count = len(strips)
    t = list(strips)
    e = [jnp.where(lanes == subs + 8 * r, 1.0, 0.0).astype(jnp.float32) for r in range(count)]
    diag = jnp.zeros((8, TILE), jnp.float32)

    def row_splat(v, i):
        return jnp.broadcast_to(v[i : i + 1, :], (8, TILE))

    def lane_splat(v, c):
        return jnp.broadcast_to(v[:, c : c + 1], (8, TILE))

    out = []
    for s in range(count):
        k = 8 * s
        last = s + 1 == count
        b = [lane_splat(t[s], k + j) for j in range(8)]
        corner = [[row_splat(b[j], i) for j in range(i + 1)] for i in range(8)]
        rt = None if last else [row_splat(t[s], i) for i in range(8)]
        re = [row_splat(e[s], i) for i in range(8)]
        l = [[None] * 8 for _ in range(8)]
        inv = []
        for j in range(8):
            iv = lax.rsqrt(corner[j][j])
            inv.append(iv)
            diag = jnp.where(lanes == k + j, corner[j][j] * iv, diag)
            for i in range(j + 1, 8):
                l[i][j] = corner[i][j] * iv
            for i in range(j + 1, 8):
                for m in range(j + 1, i + 1):
                    corner[i][m] = corner[i][m] - l[i][j] * l[m][j]
            re[j] = re[j] * iv
            if not last:
                rt[j] = rt[j] * iv
            for i in range(j + 1, 8):
                re[i] = re[i] - l[i][j] * re[j]
                if not last:
                    rt[i] = rt[i] - l[i][j] * rt[j]
        rows = re[0]
        for i in range(1, 8):
            rows = jnp.where(subs == i, re[i], rows)
        out.append(rows)
        for r in range(s + 1, count):
            c = [lane_splat(t[r], k + j) for j in range(8)]
            for j in range(8):
                c[j] = c[j] * inv[j]
                for m in range(j + 1, 8):
                    c[m] = c[m] - c[j] * l[m][j]
                t[r] = t[r] - c[j] * rt[j]
                e[r] = e[r] - c[j] * re[j]
    return out, diag[0:1, :]


def block_inverse(a_ref, x_ref, diag_ref, leaf_ref):
    steps = PB // TILE
    x_ref[...] = jnp.zeros_like(x_ref)

    def step(j, carry):
        o = pl.multiple_of(j * TILE, TILE)
        strips = [
            a_ref[pl.ds(pl.multiple_of(o + 8 * r, 8), 8), pl.ds(o, TILE)] for r in range(TILE // 8)
        ]
        rows, diag = leaf_inverse(strips)
        for r in range(TILE // 8):
            leaf_ref[8 * r : 8 * r + 8, :] = rows[r]
        diag_ref[:, pl.ds(o, TILE)] = diag
        for q in range(steps):

            @pl.when(j == q)
            def _():
                lo, hi = q * TILE, (q + 1) * TILE
                leaf = leaf_ref[...]
                x_ref[lo:hi, lo:hi] = leaf
                if q:
                    x_ref[lo:hi, 0:lo] = dot_nn(leaf, x_ref[lo:hi, 0:lo], HIGHEST)
                if q + 1 < steps:
                    p = dot_nt(a_ref[hi:PB, lo:hi], leaf, HIGHEST)
                    for b in range(q + 1, steps):
                        pb = p[(b - q - 1) * TILE :]
                        a_ref[b * TILE : PB, b * TILE : (b + 1) * TILE] -= dot_nt(pb, pb[0:TILE], HIGHEST)
                    x_ref[hi:PB, 0:hi] -= dot_nn(p, x_ref[lo:hi, 0:hi], HIGHEST)

        return carry

    lax.fori_loop(0, steps, step, 0)


def finish_panel(k, first_row, panel, inv, diag, factor_ref, wb_ref):
    w = dot_nt(panel, inv, HIGHEST)
    rows = lax.broadcasted_iota(jnp.int32, w.shape, 0) + first_row
    w = jnp.where(rows >= k * PB, w, 0.0)
    factor_ref[...] = w * (1.0 / diag)
    wb_ref[...] = w.astype(jnp.bfloat16)


def lead(ref):
    return ref[...].reshape(PB, PB)


def kernel_0(row_ref, a00, panel, inv_ref, diag_ref, factor_ref, wb_ref, a_ref, leaf_ref):
    for s in range(2):
        a_ref[s * 256 : (s + 1) * 256, :] = a00[:, s].reshape(256, PB)
    block_inverse(a_ref, inv_ref, diag_ref, leaf_ref)
    finish_panel(0, row_ref[0], panel[0], inv_ref[...], diag_ref[...], factor_ref, wb_ref)


def put_block(ref):
    return jnp.concatenate([ref[:, s].reshape(256, PB) for s in range(2)], axis=0)


def kernel_1(
    row_ref, a10, a11, panel, inv0, wb0, factor_in, inv_ref, diag_ref, factor_ref, wb_ref, lb10_ref, a_ref, leaf_ref
):
    lb10 = dot_nt(put_block(a10), inv0[...], HIGHEST).astype(jnp.bfloat16)
    lb10_ref[...] = lb10
    a_ref[...] = put_block(a11) - dot_nt(lb10, lb10)
    block_inverse(a_ref, inv_ref, diag_ref, leaf_ref)
    mine = panel[0] - dot_nt(wb0[...], lb10_ref[...])
    finish_panel(1, row_ref[0], mine, inv_ref[...], diag_ref[...], factor_ref, wb_ref)


def kernel_2(
    row_ref, a20, a21, a22, panel, inv0, inv1, lb10, wb0, wb1, factor_in, diag_ref, factor_ref, wb_ref, a_ref, leaf_ref,
    inv_ref, lb20_ref, lb21_ref
):
    lb20 = dot_nt(put_block(a20), inv0[...], HIGHEST).astype(jnp.bfloat16)
    lb20_ref[...] = lb20
    lb21 = dot_nt(put_block(a21) - dot_nt(lb20, lb10[...]), inv1[...], HIGHEST).astype(jnp.bfloat16)
    lb21_ref[...] = lb21
    a_ref[...] = put_block(a22) - dot_nt(lb20, lb20) - dot_nt(lb21, lb21)
    block_inverse(a_ref, inv_ref, diag_ref, leaf_ref)
    mine = panel[0] - dot_nt(wb0[...], lb20_ref[...]) - dot_nt(wb1[...], lb21_ref[...])
    finish_panel(2, row_ref[0], mine, inv_ref[...], diag_ref[...], factor_ref, wb_ref)


def whole(shape):
    return pl.BlockSpec(shape, lambda i: (0,) * len(shape))


def factor_step(k, first_row, front, leading, carried, factor):
    rows = front.shape[1]
    specs = [pl.BlockSpec(memory_space=pltpu.SMEM)]
    args = [first_row]
    for array, i, j in leading:
        specs.append(pl.BlockSpec((array.shape[0], 2, 8, PB), lambda _, i=i, j=j: (0, i, 0, j)))
        args.append(array)
    specs.append(pl.BlockSpec((1, rows, PB), lambda _: (0, 0, k)))
    args.append(front)
    for array in carried:
        specs.append(whole(array.shape))
        args.append(array)
    square = jax.ShapeDtypeStruct((PB, PB), jnp.float32)
    diag = jax.ShapeDtypeStruct((1, PB), jnp.float32)
    factors = jax.ShapeDtypeStruct((rows, NPIV), jnp.float32)
    wb = jax.ShapeDtypeStruct((rows, PB), jnp.bfloat16)
    factor_spec = pl.BlockSpec((rows, PB), lambda _: (0, k))
    outs = [diag, factors, wb]
    out_specs = [whole(diag.shape), factor_spec, whole(wb.shape)]
    scratch = [pltpu.VMEM((PB, PB), jnp.float32), pltpu.VMEM((TILE, TILE), jnp.float32)]
    if k < 2:
        outs.insert(0, square)
        out_specs.insert(0, whole(square.shape))
    else:
        scratch += [pltpu.VMEM((PB, PB), jnp.float32)] + [pltpu.VMEM((PB, PB), jnp.bfloat16)] * 2
    if k == 1:
        outs.append(jax.ShapeDtypeStruct((PB, PB), jnp.bfloat16))
        out_specs.append(whole((PB, PB)))
    aliases = {}
    if k:
        specs.append(pl.BlockSpec(memory_space=pl.ANY))
        args.append(factor)
        aliases = {len(args) - 1: 1 if k == 1 else 1}
        if k == 1:
            aliases = {len(args) - 1: 2}
    return pl.pallas_call(
        (kernel_0, kernel_1, kernel_2)[k],
        grid=(1,),
        in_specs=specs,
        out_specs=out_specs,
        out_shape=outs,
        scratch_shapes=scratch,
        input_output_aliases=aliases,
        compiler_params=pltpu.CompilerParams(vmem_limit_bytes=VMEM_LIMIT),
        cost_estimate=pl.CostEstimate(flops=20_000_000_000, bytes_accessed=4_000_000, transcendentals=0),
        name=f"pivot_block_{k}",
    )(*args)


def place_kernel(tiles_ref, info_ref, t0, t1, w0, w1, own, out_ref):
    i = pl.program_id(0)
    rows = own.shape[0]
    row_tile = (lax.broadcasted_iota(jnp.int32, (rows, TILE), 0) + info_ref[0] - NPIV) // TILE
    row_ids = lax.broadcasted_iota(jnp.int32, (rows, TILE), 0) + info_ref[0]
    row_live = (row_ids >= NPIV) & (row_tile < info_ref[1])
    for half, (t, w) in enumerate(((t0, w0), (t1, w1))):
        live = tiles_ref[2 * i + half] < CT
        value = t[...] - dot_nt(own[...], w[...])
        out_ref[0, :, half * TILE : (half + 1) * TILE] = jnp.where(row_live & live, value, 0.0).astype(jnp.bfloat16)


def place(tiles, info, base, own, gathered, helpers):
    rows, depth = own.shape

    def pick(half):
        return lambda i, tiles, info: (0, jnp.minimum(tiles[2 * i + half], CT - 1))

    def pick_rows(half):
        return lambda i, tiles, info: (SKIP + jnp.minimum(tiles[2 * i + half], CT - 1), 0)

    return pl.pallas_call(
        place_kernel,
        grid_spec=pltpu.PrefetchScalarGridSpec(
            num_scalar_prefetch=2,
            grid=(helpers,),
            in_specs=[
                pl.BlockSpec((rows, TILE), pick(0)),
                pl.BlockSpec((rows, TILE), pick(1)),
                pl.BlockSpec((TILE, depth), pick_rows(0)),
                pl.BlockSpec((TILE, depth), pick_rows(1)),
                pl.BlockSpec((rows, depth), lambda i, tiles, info: (0, 0)),
            ],
            out_specs=pl.BlockSpec((1, rows, 2 * TILE), lambda i, tiles, info: (i, 0, 0)),
        ),
        out_shape=jax.ShapeDtypeStruct((helpers, rows, 2 * TILE), jnp.bfloat16),
        compiler_params=pltpu.CompilerParams(vmem_limit_bytes=VMEM_LIMIT),
        name="contribution_tiles",
    )(tiles, info, base, base, gathered, gathered, own)


def assemble_kernel(tiles_ref, *refs):
    out_ref = refs[-1]
    i = pl.program_id(0)
    count = len(refs) - 1
    for half in range(count):
        live = tiles_ref[count * i + half] < CT
        value = refs[half][...].astype(jnp.float32).T
        out_ref[:, half * TILE : (half + 1) * TILE] = jnp.where(live, value, 0.0).astype(jnp.bfloat16)


def assemble(tiles, incoming, per_step=4):
    total, rows = incoming.shape

    def pick_rows(half):
        return lambda i, tiles: (SKIP + jnp.minimum(tiles[per_step * i + half], CT - 1), 0)

    return pl.pallas_call(
        assemble_kernel,
        grid_spec=pltpu.PrefetchScalarGridSpec(
            num_scalar_prefetch=1,
            grid=(PT // per_step,),
            in_specs=[pl.BlockSpec((TILE, rows), pick_rows(h)) for h in range(per_step)],
            out_specs=pl.BlockSpec((rows, per_step * TILE), lambda i, tiles: (0, i)),
        ),
        out_shape=jax.ShapeDtypeStruct((rows, total), jnp.bfloat16),
        compiler_params=pltpu.CompilerParams(vmem_limit_bytes=VMEM_LIMIT),
        name="parent_rows",
    )(tiles, *([incoming] * per_step))


def exchange(array):
    return lax.all_to_all(array, "helper", split_axis=0, concat_axis=0, tiled=True)


def local(front, tile_map, live_tiles):
    _, rows, order = front.shape
    helpers = lax.axis_size("helper")
    helper = lax.axis_index("helper")
    first_row = (helper * rows).astype(jnp.int32).reshape(1)
    piece = rows // helpers

    panel = front[0, :, :NPIV]
    scattered = exchange(panel.reshape(helpers, piece, NPIV))[: NPIV // rows]
    block_0 = exchange(
        jnp.broadcast_to(scattered[None, :2, :, :PB], (helpers, 2, piece, PB))
    )
    rest = lax.all_gather(scattered[2:], "helper", axis=0)

    moved = shifted(front[0, :, NPIV:], "front", 1)
    tiling = shifted(jnp.concatenate([tile_map[0], live_tiles]), "front", 1)
    mapping, live_count = tiling[:CT], tiling[CT]
    tile_ids = lax.iota(jnp.int32, CT)
    match = (mapping[None, :] == lax.iota(jnp.int32, PT)[:, None]) & (tile_ids[None, :] < live_count)
    tiles = jnp.where(jnp.any(match, axis=1), jnp.sum(jnp.where(match, tile_ids[None, :], 0), axis=1), CT)
    tiles = tiles.astype(jnp.int32)
    info = jnp.concatenate([first_row, live_count.reshape(1)])

    inv0, diag0, factor, wb0 = factor_step(0, first_row, front, [(block_0, 0, 0)], [], None)
    own0 = shifted(wb0, "front", 1)
    all0 = lax.all_gather(own0, "helper", axis=0, tiled=True)
    inv1, diag1, factor, wb1, lb10 = factor_step(
        1, first_row, front, [(rest, 0, 0), (rest, 0, 1)], [inv0, wb0], factor
    )
    diag2, factor, wb2 = factor_step(
        2, first_row, front, [(rest, 1, 0), (rest, 1, 1), (rest, 1, 2)], [inv0, inv1, lb10, wb0, wb1], factor
    )
    own12 = shifted(jnp.concatenate([wb1, wb2], axis=1), "front", 1)
    all12 = lax.all_gather(own12, "helper", axis=0, tiled=True)

    base = moved - dot_nt(own0, all0[NPIV:])
    outgoing = place(tiles, info, base, own12, all12, helpers)
    incoming = exchange(outgoing).reshape(order, rows)
    parent = assemble(tiles, incoming)
    diag = jnp.concatenate([diag0, diag1, diag2], axis=1)
    return factor[None], diag * diag, parent[None]


def solution(mesh):
    placed = (P("front", "helper", None), P("front", None), P("front"))
    return jax.shard_map(
        local,
        mesh=mesh,
        in_specs=placed,
        out_specs=(P("front", "helper", None), P("front", None), P("front", "helper", None)),
        check_vma=False,
    )
```

time: 1190 us -> 439 us (0.37); the launches traced: 1170 us -> 437 us
  other arithmetic: 390 us -> 2.4 us
  waiting for transfers between devices: 565 us -> 240 us
  Pallas kernels: 0 us -> 114 us
  local copies, waits for them, and re-layouts: 91.2 us -> 10.9 us
  matrix products: 45.9 us -> 10 us
  blocking collectives: 56.4 us -> 31.2 us
    another operation x52 -> x0, other arithmetic: 369 us -> none  [the longest x45 246 us: local(): chol_block = jnp.linalg.cholesky(pivot_block)]
    psum x3 -> x0, waiting for transfers between devices: 317 us -> none  [local(): lax.psum(rows_in_range(matrix[:, lower_bound:high_edge], first_row, lower...]
    all_gather x3, waiting for transfers between devices: 177 us -> 0.04 us  [the longest x1 0.02 us: local(): all0 = lax.all_gather(own0, 'helper', axis=0, tiled=True)]
    pallas_call x0 -> x5, Pallas kernels: none -> 114 us  [the longest x3 75.6 us: factor_step(): pl.pallas_call((kernel_0, kernel_1, kernel_2)[k], grid=(1,), in_specs=spe...]
    ppermute x1 -> x4, waiting for transfers between devices: 71.2 us -> 167 us  [shifted(): lax.ppermute(array, axis, [(i, (i + by) % count) for i in range(count)])]
    all_to_all x0 -> x2, waiting for transfers between devices: none -> 72.8 us  [exchange(): lax.all_to_all(array, 'helper', split_axis=0, concat_axis=0, tiled=True)]
    all_to_all x1, blocking collectives: 56.4 us -> 31.2 us  [exchange(): lax.all_to_all(array, 'helper', split_axis=0, concat_axis=0, tiled=True)]
    another operation x52 -> x1, local copies, waits for them, and re-layouts: 24.5 us -> 1.51 us  [local(): scattered = exchange(panel.reshape(helpers, piece, NPIV))[:NPIV // rows]]
  transfers between devices with their start and end apart: 7 -> 9, of which waited for: 7 -> 5; matrix products, arithmetic and copies ran while one was open for 2% -> 4% of each run, Pallas kernels for 0% -> 17%
where the time goes in v1:
time: 439 us; the launch traced here: 437 us
  waiting for transfers between devices  240 us (55%)
  Pallas kernels  114 us (26%)
  blocking collectives  31.2 us (7%)
  between operations  14.5 us (3%)
  starting transfers between devices  13.8 us (3%)
  local copies, waits for them, and re-layouts  10.9 us (2%)
  matrix products  10 us (2%)
    ppermute x4, waiting for transfers between devices, shifted(): lax.ppermute(array, axis, [(i, (i + by) % count) for i in range(count)])  167 us
    pallas_call x3, Pallas kernels, factor_step(): pl.pallas_call((kernel_0, kernel_1, kernel_2)[k], grid=(1,), in_specs=spe...  75.6 us
    all_to_all x2, waiting for transfers between devices, exchange(): lax.all_to_all(array, 'helper', split_axis=0, concat_axis=0, tiled=True)  72.8 us
    all_to_all x1, blocking collectives, exchange(): lax.all_to_all(array, 'helper', split_axis=0, concat_axis=0, tiled=True)  31.2 us
    pallas_call x1, Pallas kernels, place(): pl.pallas_call(place_kernel, grid_spec=pltpu.PrefetchScalarGridSpec(num_s...  27.2 us
    pallas_call x1, Pallas kernels, assemble(): pl.pallas_call(assemble_kernel, grid_spec=pltpu.PrefetchScalarGridSpec(nu...  11.4 us
    all_to_all x2, starting transfers between devices, exchange(): lax.all_to_all(array, 'helper', split_axis=0, concat_axis=0, tiled=True)  11.2 us
    dot_general x1, matrix products, dot_nt(): lax.dot_general(a, b, (((1,), (1,)), ((), ())), precision=precision, pref...  10 us
  transfers between devices with their start and end apart: 9, of which 5 were waited for; matrix products, arithmetic and copies ran while one was open for 4% of the time, Pallas kernels for 17%

profile of v1, /device:TPU:0, one launch (start us, length us, event | category | flops | bytes accessed | tf_op | source)
XLA Modules:
  0.0 437.3 jit_solution(5964358425151789863)
XLA Ops:
  7.2 0.0 all-gather.9.cloned.1.call-start
  7.2 1.5 slice_bitcast_fusion.1
  8.7 31.2 %all_to_all.15 = f32[32,8,1536]{2,1,0:T(8,128)S(1)} all-to-all(f32[32,8,1536]{2,1,0:T(8,128)S(1)} %slice_bitcast_fusion.1), channel_id=1, replica_groups=mesh['front'=4,'helper'=32] {'helper'}, dimensions={0} | all-to-all | bytes 3145728 | tf_op jit(solution)/shard_map/all_to_all | solution.py:300
  39.9 0.7 slice.31
  40.6 0.0 all-gather.9.cloned.1.call-update
  40.7 1.1 broadcast_in_dim.32
  41.8 3.9 all-to-all-start.1
  45.7 0.0 all-gather.5.cloned.1.call-start
  45.8 19.9 %all-to-all-done.1.a00 = f32[32,2,8,512]{3,2,1,0:T(8,128)S(1)} async-done(((f32[32,2,8,512]{3,2,1,0:T(8,128)}), f32[32,2,8,512]{3,2,1,0:T(8,128)S(1)}, u32[]{:S(2)}, u32[]{:S(2)}) %all-to-all-start.1) | async-done | bytes 1048608 | tf_op jit(solution)/shard_map/all_to_all | solution.py:300
  65.7 22.2 %pivot_block_0.1 = (f32[512,512]{1,0:T(8,128)S(1)}, f32[1,512]{1,0:T(1,128)S(1)}, f32[256,1536]{1,0:T(8,128)}, bf16[256,512]{1,0:T(8,128)(2,1)S(1)}) custom-call(s32[1]{0:T(128)} %bitcast.row_ref, f32[32,2,8,512]{3,2,1,0:T(8,128)S(1)} %all-to-all-done.1.a00, f32[1,256,8192]{2,1,0:T(8,128)} %panel.5), custom_call_target="tpu_custom_call" | custom-call | flops 20000000000 | bytes 4000000 | tf_op jit(solution)/shard_map/pivot_block_0/pallas_call | solution.py:214
  87.9 1.5 collective-permute-start.2
  89.4 7.5 %collective-permute-done.2 = bf16[256,512]{1,0:T(8,128)(2,1)S(1)} collective-permute-done((bf16[256,512]{1,0:T(8,128)(2,1)S(1)}, bf16[256,512]{1,0:T(8,128)(2,1)S(1)}, u32[]{:S(2)}, u32[]{:S(2)}) %collective-permute-start.2) | collective-permute-done | bytes 262176 | tf_op jit(solution)/shard_map/ppermute | solution.py:23
  96.8 0.0 copy-start.3
  96.9 0.7 copy-done.3
  97.6 0.0 all-gather.5.cloned.1.call-update
  97.6 0.0 all-gather.7.cloned.1.call-start
  97.6 0.0 all-gather.9.cloned.1.call-done
  97.7 25.4 %pivot_block_1.1 = (f32[512,512]{1,0:T(8,128)S(1)}, f32[1,512]{1,0:T(1,128)S(1)}, f32[256,1536]{1,0:T(8,128)}, bf16[256,512]{1,0:T(8,128)(2,1)S(1)}, bf16[512,512]{1,0:T(8,128)(2,1)S(1)}) custom-call(s32[1]{0:T(128)} %bitcast.row_ref, f32[32,4,8,1536]{3,2,1,0:T(8,128)} %bitcast.14, f32[32,4,8,1536]{3,2,1,0:T(8,128)} %bitcast.15, ...), custom_call_target="tpu_custom_call", output_to_operand_aliasing={{2}: (6, {})} | custom-call | flops 20000000000 | bytes 4000000 | tf_op jit(solution)/shard_map/pivot_block_1/pallas_call | solution.py:214
  123.1 28.0 %pivot_block_2.1 = (f32[1,512]{1,0:T(1,128)S(1)}, f32[256,1536]{1,0:T(8,128)}, bf16[256,512]{1,0:T(8,128)(2,1)S(1)}) custom-call(s32[1]{0:T(128)} %bitcast.row_ref, f32[32,4,8,1536]{3,2,1,0:T(8,128)} %bitcast.16, f32[32,4,8,1536]{3,2,1,0:T(8,128)} %bitcast.17, f32[32,4,8,1536]{3,2,1,0:T(8,128)} %bitcast.18, ...), custom_call_target="tpu_custom_call", output_to_operand_aliasing={{1}: (10, {})} | custom-call | flops 20000000000 | bytes 4000000 | tf_op jit(solution)/shard_map/pivot_block_2/pallas_call | solution.py:214
  151.1 0.1 pad_maximum_fusion
  151.2 0.3 collective-permute-start.3
  151.5 13.4 %collective-permute-done.3.own = bf16[256,1024]{1,0:T(8,128)(2,1)S(1)} collective-permute-done((bf16[256,1024]{1,0:T(8,128)(2,1)S(1)}, bf16[256,1024]{1,0:T(8,128)(2,1)S(1)}, u32[]{:S(2)}, u32[]{:S(2)}) %collective-permute-start.3) | collective-permute-done | bytes 524320 | tf_op jit(solution)/shard_map/ppermute | solution.py:23
  164.9 0.0 copy-start.1
  164.9 0.8 copy-done.1
  165.7 0.0 all-gather.7.cloned.1.call-update
  165.7 0.0 copy-start.5
  165.7 0.0 copy-start.4
  165.7 3.4 slice_bitcast_fusion
  169.2 0.1 collective-permute-start.1
  169.9 0.0 copy-done.5
  169.9 0.1 pad_add_fusion
  170.0 0.5 collective-permute-start
  170.5 146.4 %collective-permute-done = s32[53]{0:T(128)S(1)} collective-permute-done((s32[53]{0:T(128)S(1)}, s32[53]{0:T(128)S(1)}, u32[]{:S(2)}, u32[]{:S(2)}) %collective-permute-start) | collective-permute-done | bytes 244 | tf_op jit(solution)/shard_map/ppermute | solution.py:23
  316.9 0.7 slice.28
  317.5 0.8 pad_add_fusion.1.info_ref
  318.3 0.7 iota_compare_fusion.1
  319.0 0.1 fusion.2
  319.1 0.1 select_reduce_fusion
  319.2 0.0 copy-start.2
  319.2 0.0 collective-permute-done.1
  319.3 0.0 all-gather.5.cloned.1.call-done
  319.3 0.0 copy-done.4
  319.3 10.0 %convolution_subtract_fusion.t0.t1 = f32[256,6656]{1,0:T(8,128)} fusion(f32[256,6656]{1,0:T(8,128)} %collective-permute-done.1, bf16[256,512]{1,0:T(8,128)(2,1)S(1)} %copy-done.4, bf16[8192,512]{1,0:T(8,128)(2,1)} %all-gather.5.cloned.1.call-done), kind=kOutput, calls=%fused_computation | convolution fusion | flops 1746534400 | bytes 20709376 | tf_op jit(solution)/shard_map/dot_general | solution.py:27
  329.3 0.0 all-gather.7.cloned.1.call-done.w0.w1
  329.3 0.0 copy-done.2
  329.3 27.2 %contribution_tiles.1 = bf16[32,256,256]{2,1,0:T(8,128)(2,1)S(1)} custom-call(s32[64]{0:T(128)S(1)} %broadcast_select_fusion.tiles_ref, s32[2]{0:T(128)S(1)} %pad_add_fusion.1.info_ref, f32[256,6656]{1,0:T(8,128)} %convolution_subtract_fusion.t0.t1, f32[256,6656]{1,0:T(8,128)} %convolution_subtract_fusion.t0.t1, ...), custom_call_target="tpu_custom_call" | custom-call | tf_op jit(solution)/shard_map/contribution_tiles/pallas_call | solution.py:249
  356.6 0.0 copy-start
  356.6 2.0 copy-done
  358.6 7.3 %all-to-all-start.2 = ((bf16[32,256,256]{2,1,0:T(8,128)(2,1)}), bf16[32,256,256]{2,1,0:T(8,128)(2,1)}, u32[]{:S(2)}, u32[]{:S(2)}) async-start(bf16[32,256,256]{2,1,0:T(8,128)(2,1)} %copy-done), calls=%async_computation.2 | async-start | bytes 8388608 | tf_op jit(solution)/shard_map/all_to_all | solution.py:300
  365.9 0.6 maximum_multiply_fusion
  366.5 52.9 %all-to-all-done.2 = bf16[32,256,256]{2,1,0:T(8,128)(2,1)} async-done(((bf16[32,256,256]{2,1,0:T(8,128)(2,1)}), bf16[32,256,256]{2,1,0:T(8,128)(2,1)}, u32[]{:S(2)}, u32[]{:S(2)}) %all-to-all-start.2) | async-done | bytes 4194336 | tf_op jit(solution)/shard_map/all_to_all | solution.py:300
  419.4 11.4 %parent_rows.1 = bf16[256,8192]{1,0:T(8,128)(2,1)} custom-call(s32[64]{0:T(128)S(1)} %broadcast_select_fusion.tiles_ref, bf16[8192,256]{1,0:T(8,128)(2,1)} %bitcast.7.refs_0_.refs_1_.refs_2_.refs_3_, bf16[8192,256]{1,0:T(8,128)(2,1)} %bitcast.7.refs_0_.refs_1_.refs_2_.refs_3_, bf16[8192,256]{1,0:T(8,128)(2,1)} %bitcast.7.refs_0_.refs_1_.refs_2_.refs_3_, ...), custom_call_target="tpu_custom_call" | custom-call | tf_op jit(solution)/shard_map/parent_rows/pallas_call | solution.py:285
  (2 shorter events, 0.0 us)
Async XLA Ops:
  7.2 90.5 %all-gather.9.cloned.1.call-start = ((), (), s32[]{:S(2)}) async-start(), calls=%async_computation.5 | async-start | bytes 6488064 | tf_op jit(solution)/shard_map/all_gather | solution.py:315
  41.8 23.9 %all-to-all-start.1 = ((f32[32,2,8,512]{3,2,1,0:T(8,128)}), f32[32,2,8,512]{3,2,1,0:T(8,128)S(1)}, u32[]{:S(2)}, u32[]{:S(2)}) async-start(f32[32,2,8,512]{3,2,1,0:T(8,128)} %broadcast_in_dim.32), calls=%async_computation.1 | async-start | bytes 2097152 | tf_op jit(solution)/shard_map/all_to_all | solution.py:300
  45.7 273.6 %all-gather.5.cloned.1.call-start = ((), (), s32[]{:S(2)}) async-start(), calls=%async_computation.3 | async-start | bytes 8650752 | tf_op jit(solution)/shard_map/all_gather | solution.py:328
  87.9 9.0 %collective-permute-start.2 = (bf16[256,512]{1,0:T(8,128)(2,1)S(1)}, bf16[256,512]{1,0:T(8,128)(2,1)S(1)}, u32[]{:S(2)}, u32[]{:S(2)}) collective-permute-start(bf16[256,512]{1,0:T(8,128)(2,1)S(1)} %get-tuple-element.16.wb0), channel_id=1, source_target_pairs={{0,32},{32,64},{64,96},{96,0},{1,33},{33,65},{65,97},{97,1},{2,34}... | collective-permute-start | bytes 786440 | tf_op jit(solution)/shard_map/ppermute | solution.py:23
  96.8 0.7 copy-start.3
  97.6 231.8 %all-gather.7.cloned.1.call-start = ((), (), s32[]{:S(2)}) async-start(), calls=%async_computation.4 | async-start | bytes 17301504 | tf_op jit(solution)/shard_map/all_gather | solution.py:336
  151.2 13.7 %collective-permute-start.3 = (bf16[256,1024]{1,0:T(8,128)(2,1)S(1)}, bf16[256,1024]{1,0:T(8,128)(2,1)S(1)}, u32[]{:S(2)}, u32[]{:S(2)}) collective-permute-start(bf16[256,1024]{1,0:T(8,128)(2,1)S(1)} %pad_maximum_fusion), channel_id=1, source_target_pairs={{0,32},{32,64},{64,96},{96,0},{1,33},{33,65},{65,97},{97,1},{2,34}... | collective-permute-start | bytes 1572872 | tf_op jit(solution)/shard_map/ppermute | solution.py:23
  164.9 0.8 copy-start.1
  165.7 4.2 copy-start.5
  165.7 153.6 %copy-start.4 = (bf16[256,512]{1,0:T(8,128)(2,1)S(1)}, bf16[256,512]{1,0:T(8,128)(2,1)}, u32[]{:S(2)}) copy-start(bf16[256,512]{1,0:T(8,128)(2,1)} %copy-done.3) | copy-start | bytes 786436
  169.2 150.1 %collective-permute-start.1 = (f32[256,6656]{1,0:T(8,128)S(1)}, f32[256,6656]{1,0:T(8,128)}, u32[]{:S(2)}, u32[]{:S(2)}) collective-permute-start(f32[256,6656]{1,0:T(8,128)S(1)} %slice_bitcast_fusion), channel_id=1, source_target_pairs={{0,32},{32,64},{64,96},{96,0},{1,33},{33,65},{65,97},{97,1},{2,34}... | collective-permute-start | bytes 20447240 | tf_op jit(solution)/shard_map/ppermute | solution.py:23
  170.0 146.9 %collective-permute-start = (s32[53]{0:T(128)S(1)}, s32[53]{0:T(128)S(1)}, u32[]{:S(2)}, u32[]{:S(2)}) collective-permute-start(s32[53]{0:T(128)S(1)} %pad_add_fusion), channel_id=1, source_target_pairs={{0,32},{32,64},{64,96},{96,0},{1,33},{33,65},{65,97},{97,1},{2,34}... | collective-permute-start | bytes 644 | tf_op jit(solution)/shard_map/ppermute | solution.py:23
  319.2 10.1 %copy-start.2 = (bf16[256,1024]{1,0:T(8,128)(2,1)S(1)}, bf16[256,1024]{1,0:T(8,128)(2,1)}, u32[]{:S(2)}) copy-start(bf16[256,1024]{1,0:T(8,128)(2,1)} %copy-done.1) | copy-start | bytes 1572868
  356.6 2.0 copy-start
  358.6 60.8 %all-to-all-start.2 = ((bf16[32,256,256]{2,1,0:T(8,128)(2,1)}), bf16[32,256,256]{2,1,0:T(8,128)(2,1)}, u32[]{:S(2)}, u32[]{:S(2)}) async-start(bf16[32,256,256]{2,1,0:T(8,128)(2,1)} %copy-done), calls=%async_computation.2 | async-start | bytes 8388608 | tf_op jit(solution)/shard_map/all_to_all | solution.py:300
Sparse Core Ops, SparseCore 0:
  40.8 52.5 all-gather.8
  97.7 49.9 all-gather.4
  165.8 69.7 all-gather.6

commit v2 on v1

--- a/solution.py
+++ b/solution.py
@@ -15,6 +15,7 @@
 PT = 64
 SKIP = NPIV // TILE
 VMEM_LIMIT = 48 << 20
+CHUNKS = (32, 32, 40, 48, 104)
 HIGHEST = lax.Precision.HIGHEST
 
 
@@ -208,9 +209,7 @@
     if k:
         specs.append(pl.BlockSpec(memory_space=pl.ANY))
         args.append(factor)
-        aliases = {len(args) - 1: 1 if k == 1 else 1}
-        if k == 1:
-            aliases = {len(args) - 1: 2}
+        aliases = {len(args) - 1: 2 if k == 1 else 1}
     return pl.pallas_call(
         (kernel_0, kernel_1, kernel_2)[k],
         grid=(1,),
@@ -225,75 +224,131 @@
     )(*args)
 
 
-def place_kernel(tiles_ref, info_ref, t0, t1, w0, w1, own, out_ref):
+def cut_kernel(front, *outs):
+    start = 0
+    for out in outs:
+        count = out.shape[0]
+        out[...] = front[0, start : start + count, :]
+        start += count
+
+
+def cut(front, chunks):
+    rows, width = front.shape[1], front.shape[2] - NPIV
+    return pl.pallas_call(
+        cut_kernel,
+        grid=(width // PB,),
+        in_specs=[pl.BlockSpec((1, rows, PB), lambda i: (0, 0, NPB + i))],
+        out_specs=[pl.BlockSpec((c, PB), lambda i: (0, i)) for c in chunks],
+        out_shape=[jax.ShapeDtypeStruct((c, width), jnp.float32) for c in chunks],
+        compiler_params=pltpu.CompilerParams(vmem_limit_bytes=VMEM_LIMIT),
+        name="cut_rows",
+    )(front)
+
+
+def transposed_base_kernel(w, own, *refs):
+    chunks, (out_ref, own_ref) = refs[:-2], refs[-2:]
+
+    @pl.when(pl.program_id(0) == 0)
+    def _():
+        own_ref[...] = own[...].T
+
+    entries = jnp.concatenate([c[...] for c in chunks], axis=0)
+    out_ref[...] = entries.T - dot_nn(w[...], own_ref[...])
+
+
+def transposed_base(chunks, own, gathered):
+    rows, depth = own.shape
+    width = chunks[0].shape[1]
+    return pl.pallas_call(
+        transposed_base_kernel,
+        grid=(width // PB,),
+        in_specs=[pl.BlockSpec((PB, depth), lambda i: (NPB + i, 0)), whole(own.shape)]
+        + [pl.BlockSpec((c.shape[0], PB), lambda i: (0, i)) for c in chunks],
+        out_specs=pl.BlockSpec((PB, rows), lambda i: (i, 0)),
+        out_shape=jax.ShapeDtypeStruct((width, rows), jnp.float32),
+        scratch_shapes=[pltpu.VMEM((depth, rows), jnp.bfloat16)],
+        compiler_params=pltpu.CompilerParams(vmem_limit_bytes=VMEM_LIMIT),
+        name="transposed_base",
+    )(gathered, own, *chunks)
+
+
+def contribution_kernel(target_ref, info_ref, base, w, own, out_ref, own_ref):
     i = pl.program_id(0)
     rows = own.shape[0]
-    row_tile = (lax.broadcasted_iota(jnp.int32, (rows, TILE), 0) + info_ref[0] - NPIV) // TILE
-    row_ids = lax.broadcasted_iota(jnp.int32, (rows, TILE), 0) + info_ref[0]
-    row_live = (row_ids >= NPIV) & (row_tile < info_ref[1])
-    for half, (t, w) in enumerate(((t0, w0), (t1, w1))):
-        live = tiles_ref[2 * i + half] < CT
-        value = t[...] - dot_nt(own[...], w[...])
-        out_ref[0, :, half * TILE : (half + 1) * TILE] = jnp.where(row_live & live, value, 0.0).astype(jnp.bfloat16)
-
-
-def place(tiles, info, base, own, gathered, helpers):
-    rows, depth = own.shape
-
-    def pick(half):
-        return lambda i, tiles, info: (0, jnp.minimum(tiles[2 * i + half], CT - 1))
-
-    def pick_rows(half):
-        return lambda i, tiles, info: (SKIP + jnp.minimum(tiles[2 * i + half], CT - 1), 0)
+
+    @pl.when(i == 0)
+    def _():
+        own_ref[...] = own[...].T
+        out_ref[...] = jnp.zeros_like(out_ref)
+
+    ids = lax.broadcasted_iota(jnp.int32, (TILE, rows), 1) + info_ref[0]
+    keep = (ids >= NPIV) & (ids < NPIV + info_ref[1] * TILE)
+    value = base[...] - dot_nn(w[...], own_ref[...])
+    count = value.shape[0] // TILE
+    for n in range(count):
+
+        @pl.when(count * i + n < info_ref[1])
+        def _():
+            target = target_ref[count * i + n]
+            at = pl.multiple_of(target % 2 * TILE, TILE)
+            tile = jnp.where(keep, value[n * TILE : (n + 1) * TILE], 0.0)
+            out_ref[target // 2, pl.ds(at, TILE), :] = tile.astype(jnp.bfloat16)
+
+
+def contributions(targets, info, base, own, gathered):
+    width, rows = base.shape
+    depth = own.shape[1]
+    return pl.pallas_call(
+        contribution_kernel,
+        grid_spec=pltpu.PrefetchScalarGridSpec(
+            num_scalar_prefetch=2,
+            grid=(width // PB,),
+            in_specs=[
+                pl.BlockSpec((PB, rows), lambda i, target, info: (i, 0)),
+                pl.BlockSpec((PB, depth), lambda i, target, info: (NPB + i, 0)),
+                pl.BlockSpec((rows, depth), lambda i, target, info: (0, 0)),
+            ],
+            out_specs=pl.BlockSpec((PT // 2, 2 * TILE, rows), lambda i, target, info: (0, 0, 0)),
+            scratch_shapes=[pltpu.VMEM((depth, rows), jnp.bfloat16)],
+        ),
+        out_shape=jax.ShapeDtypeStruct((PT // 2, 2 * TILE, rows), jnp.bfloat16),
+        compiler_params=pltpu.CompilerParams(vmem_limit_bytes=VMEM_LIMIT),
+        name="contributions",
+    )(targets, info, base, gathered, own)
+
+
+def place_kernel(source_ref, *refs):
+    tiles, out_ref = refs[:-1], refs[-1]
+    i = pl.program_id(0)
+    for n, tile in enumerate(tiles):
+        live = source_ref[len(tiles) * i + n] < CT
+        out_ref[:, n * TILE : (n + 1) * TILE] = jnp.where(live, tile[0], jnp.zeros_like(tile[0]))
+
+
+def place(sources, incoming, per_step=8):
+    _, width, rows = incoming.shape
+    skip = NPIV // rows
+    each = rows // TILE
+
+    def pick(n):
+        def index(i, source):
+            tile = jnp.minimum(source[per_step * i + n], CT - 1)
+            return skip + tile // each, 0, tile % each
+
+        return index
 
     return pl.pallas_call(
         place_kernel,
         grid_spec=pltpu.PrefetchScalarGridSpec(
-            num_scalar_prefetch=2,
-            grid=(helpers,),
-            in_specs=[
-                pl.BlockSpec((rows, TILE), pick(0)),
-                pl.BlockSpec((rows, TILE), pick(1)),
-                pl.BlockSpec((TILE, depth), pick_rows(0)),
-                pl.BlockSpec((TILE, depth), pick_rows(1)),
-                pl.BlockSpec((rows, depth), lambda i, tiles, info: (0, 0)),
-            ],
-            out_specs=pl.BlockSpec((1, rows, 2 * TILE), lambda i, tiles, info: (i, 0, 0)),
-        ),
-        out_shape=jax.ShapeDtypeStruct((helpers, rows, 2 * TILE), jnp.bfloat16),
-        compiler_params=pltpu.CompilerParams(vmem_limit_bytes=VMEM_LIMIT),
-        name="contribution_tiles",
-    )(tiles, info, base, base, gathered, gathered, own)
-
-
-def assemble_kernel(tiles_ref, *refs):
-    out_ref = refs[-1]
-    i = pl.program_id(0)
-    count = len(refs) - 1
-    for half in range(count):
-        live = tiles_ref[count * i + half] < CT
-        value = refs[half][...].astype(jnp.float32).T
-        out_ref[:, half * TILE : (half + 1) * TILE] = jnp.where(live, value, 0.0).astype(jnp.bfloat16)
-
-
-def assemble(tiles, incoming, per_step=4):
-    total, rows = incoming.shape
-
-    def pick_rows(half):
-        return lambda i, tiles: (SKIP + jnp.minimum(tiles[per_step * i + half], CT - 1), 0)
-
-    return pl.pallas_call(
-        assemble_kernel,
-        grid_spec=pltpu.PrefetchScalarGridSpec(
             num_scalar_prefetch=1,
             grid=(PT // per_step,),
-            in_specs=[pl.BlockSpec((TILE, rows), pick_rows(h)) for h in range(per_step)],
-            out_specs=pl.BlockSpec((rows, per_step * TILE), lambda i, tiles: (0, i)),
+            in_specs=[pl.BlockSpec((1, width, TILE), pick(n)) for n in range(per_step)],
+            out_specs=pl.BlockSpec((width, per_step * TILE), lambda i, source: (0, i)),
         ),
-        out_shape=jax.ShapeDtypeStruct((rows, total), jnp.bfloat16),
+        out_shape=jax.ShapeDtypeStruct((width, PT * TILE), jnp.bfloat16),
         compiler_params=pltpu.CompilerParams(vmem_limit_bytes=VMEM_LIMIT),
         name="parent_rows",
-    )(tiles, *([incoming] * per_step))
+    )(sources, *([incoming] * per_step))
 
 
 def exchange(array):
@@ -307,40 +362,59 @@
     first_row = (helper * rows).astype(jnp.int32).reshape(1)
     piece = rows // helpers
 
+    chunks = cut(front, CHUNKS)
+
     panel = front[0, :, :NPIV]
     scattered = exchange(panel.reshape(helpers, piece, NPIV))[: NPIV // rows]
-    block_0 = exchange(
-        jnp.broadcast_to(scattered[None, :2, :, :PB], (helpers, 2, piece, PB))
-    )
+    scattered, *chunks = lax.optimization_barrier((scattered, *chunks))
+    block_0 = exchange(jnp.broadcast_to(scattered[None, :2, :, :PB], (helpers, 2, piece, PB)))
     rest = lax.all_gather(scattered[2:], "helper", axis=0)
-
-    moved = shifted(front[0, :, NPIV:], "front", 1)
+    chunks[0] = shifted(chunks[0], "front", 1)
+
     tiling = shifted(jnp.concatenate([tile_map[0], live_tiles]), "front", 1)
-    mapping, live_count = tiling[:CT], tiling[CT]
-    tile_ids = lax.iota(jnp.int32, CT)
-    match = (mapping[None, :] == lax.iota(jnp.int32, PT)[:, None]) & (tile_ids[None, :] < live_count)
-    tiles = jnp.where(jnp.any(match, axis=1), jnp.sum(jnp.where(match, tile_ids[None, :], 0), axis=1), CT)
-    tiles = tiles.astype(jnp.int32)
+    targets, live_count = tiling[:CT], tiling[CT]
+    sources = tile_sources(targets, live_count)
     info = jnp.concatenate([first_row, live_count.reshape(1)])
 
+    block_0, *chunks = lax.optimization_barrier((block_0, *chunks))
     inv0, diag0, factor, wb0 = factor_step(0, first_row, front, [(block_0, 0, 0)], [], None)
+    chunks[1] = shifted(chunks[1], "front", 1)
+
+    wb0, *chunks = lax.optimization_barrier((wb0, *chunks))
     own0 = shifted(wb0, "front", 1)
+    inv0, own0, *chunks = lax.optimization_barrier((inv0, own0, *chunks))
     all0 = lax.all_gather(own0, "helper", axis=0, tiled=True)
     inv1, diag1, factor, wb1, lb10 = factor_step(
         1, first_row, front, [(rest, 0, 0), (rest, 0, 1)], [inv0, wb0], factor
     )
+    chunks[2] = shifted(chunks[2], "front", 1)
+
+    inv1, wb1, *chunks = lax.optimization_barrier((inv1, wb1, *chunks))
     diag2, factor, wb2 = factor_step(
         2, first_row, front, [(rest, 1, 0), (rest, 1, 1), (rest, 1, 2)], [inv0, inv1, lb10, wb0, wb1], factor
     )
-    own12 = shifted(jnp.concatenate([wb1, wb2], axis=1), "front", 1)
+    own1 = shifted(wb1, "front", 1)
+    chunks[3] = shifted(chunks[3], "front", 1)
+
+    wb2, own1, *chunks = lax.optimization_barrier((wb2, own1, *chunks))
+    own2 = shifted(wb2, "front", 1)
+    own2, *chunks = lax.optimization_barrier((own2, *chunks))
+    own12 = jnp.concatenate([own1, own2], axis=1)
     all12 = lax.all_gather(own12, "helper", axis=0, tiled=True)
-
-    base = moved - dot_nt(own0, all0[NPIV:])
-    outgoing = place(tiles, info, base, own12, all12, helpers)
-    incoming = exchange(outgoing).reshape(order, rows)
-    parent = assemble(tiles, incoming)
+    chunks[4] = shifted(chunks[4], "front", 1)
+
+    base = transposed_base(chunks, own0, all0)
+    outgoing = contributions(targets, info, base, own12, all12)
+    parent = place(sources, exchange(outgoing))
     diag = jnp.concatenate([diag0, diag1, diag2], axis=1)
     return factor[None], diag * diag, parent[None]
+
+
+def tile_sources(mapping, live_count):
+    tile_ids = lax.iota(jnp.int32, CT)[None, :]
+    match = (mapping[None, :] == lax.iota(jnp.int32, PT)[:, None]) & (tile_ids < live_count)
+    found = jnp.sum(jnp.where(match, tile_ids + 1, 0), axis=1)
+    return jnp.where(found > 0, found - 1, CT).astype(jnp.int32)
 
 
 def solution(mesh):

time: 439 us -> 345 us (0.79)
  waiting for transfers between devices: 240 us -> 162 us
  blocking collectives: 31.2 us -> 0 us
  starting transfers between devices: 13.8 us -> 26.9 us
  matrix products: 10 us -> 0 us
  local copies, waits for them, and re-layouts: 10.9 us -> 19 us
  Pallas kernels: 114 us -> 119 us
    ppermute x4 -> x9, waiting for transfers between devices: 167 us -> 98.2 us  [shifted(): lax.ppermute(array, axis, [(i, (i + by) % count) for i in range(count)])]
    all_to_all x1 -> x0, blocking collectives: 31.2 us -> none  [exchange(): lax.all_to_all(array, 'helper', split_axis=0, concat_axis=0, tiled=True)]
    pallas_call x1 -> x3, Pallas kernels: 11.4 us -> 36.3 us  [the longest x1 14.6 us: contributions(): pl.pallas_call(contribution_kernel, grid_spec=pltpu.PrefetchScalarGridSpe...]
    pallas_call x1, Pallas kernels: 27.2 us -> 7.51 us  [place(): pl.pallas_call(place_kernel, grid_spec=pltpu.PrefetchScalarGridSpec(num_s...]
    unnamed x12 -> x37, local copies, waits for them, and re-layouts: 3.52 us -> 13.9 us
    dot_general x1 -> x0, matrix products: 10 us -> none  [dot_nt(): lax.dot_general(a, b, (((1,), (1,)), ((), ())), precision=precision, pref...]
    all_to_all x2 -> x3, waiting for transfers between devices: 72.8 us -> 63.8 us  [exchange(): lax.all_to_all(array, 'helper', split_axis=0, concat_axis=0, tiled=True)]
    all_to_all x2 -> x3, starting transfers between devices: 11.2 us -> 19.8 us  [exchange(): lax.all_to_all(array, 'helper', split_axis=0, concat_axis=0, tiled=True)]
  transfers between devices with their start and end apart: 9 -> 15, of which waited for: 5 -> 7; matrix products, arithmetic and copies ran while one was open for 4% -> 1% of each run, Pallas kernels for 17% -> 28%
where the time goes in v2:
time: 345 us; the launch traced here: 344 us
  waiting for transfers between devices  162 us (47%)
  Pallas kernels  119 us (34%)
  starting transfers between devices  26.9 us (8%)
  local copies, waits for them, and re-layouts  19 us (6%)
  between operations  14.6 us (4%)
    ppermute x9, waiting for transfers between devices, shifted(): lax.ppermute(array, axis, [(i, (i + by) % count) for i in range(count)])  98.2 us
    pallas_call x3, Pallas kernels, factor_step(): pl.pallas_call((kernel_0, kernel_1, kernel_2)[k], grid=(1,), in_specs=spe...  75.4 us
    all_to_all x3, waiting for transfers between devices, exchange(): lax.all_to_all(array, 'helper', split_axis=0, concat_axis=0, tiled=True)  63.8 us
    all_to_all x3, starting transfers between devices, exchange(): lax.all_to_all(array, 'helper', split_axis=0, concat_axis=0, tiled=True)  19.8 us
    pallas_call x1, Pallas kernels, contributions(): pl.pallas_call(contribution_kernel, grid_spec=pltpu.PrefetchScalarGridSpe...  14.6 us
    unnamed x37, local copies, waits for them, and re-layouts  13.9 us
    pallas_call x1, Pallas kernels, transposed_base(): pl.pallas_call(transposed_base_kernel, grid=(width // PB,), in_specs=[pl....  12.4 us
    pallas_call x1, Pallas kernels, cut(): pl.pallas_call(cut_kernel, grid=(width // PB,), in_specs=[pl.BlockSpec((1...  9.27 us
  transfers between devices with their start and end apart: 15, of which 7 were waited for; matrix products, arithmetic and copies ran while one was open for 1% of the time, Pallas kernels for 28%

profile of v2, /device:TPU:0, one launch (start us, length us, event | category | flops | bytes accessed | tf_op | source)
XLA Modules:
  0.0 343.9 jit_solution(8940036885476096520)
XLA Ops:
  7.2 2.7 slice_bitcast_fusion
  9.8 8.4 %all-to-all-start = ((f32[32,8,1536]{2,1,0:T(8,128)}), f32[32,8,1536]{2,1,0:T(8,128)S(1)}, u32[]{:S(2)}, u32[]{:S(2)}) async-start(f32[32,8,1536]{2,1,0:T(8,128)} %slice_bitcast_fusion), calls=%async_computation | async-start | bytes 3145728 | tf_op jit(solution)/shard_map/all_to_all | solution.py:355
  18.2 0.0 all-gather.9.cloned.1.call-start
  18.3 9.3 %cut_rows.1 = (f32[32,6656]{1,0:T(8,128)S(1)}, f32[32,6656]{1,0:T(8,128)S(1)}, f32[40,6656]{1,0:T(8,128)S(1)}, f32[48,6656]{1,0:T(8,128)S(1)}, f32[104,6656]{1,0:T(8,128)}) custom-call(f32[1,256,8192]{2,1,0:T(8,128)} %panel.5), custom_call_target="tpu_custom_call" | custom-call | tf_op jit(solution)/shard_map/cut_rows/pallas_call | solution.py:237
  27.6 1.0 copy-done.9
  28.6 0.9 copy-done.11
  29.5 1.0 copy-done.12
  30.5 11.7 %all-to-all-done = f32[32,8,1536]{2,1,0:T(8,128)S(1)} async-done(((f32[32,8,1536]{2,1,0:T(8,128)}), f32[32,8,1536]{2,1,0:T(8,128)S(1)}, u32[]{:S(2)}, u32[]{:S(2)}) %all-to-all-start) | async-done | bytes 1572896 | tf_op jit(solution)/shard_map/all_to_all | solution.py:355
  42.2 0.7 slice.20
  42.9 0.0 all-gather.9.cloned.1.call-update
  42.9 1.1 broadcast_in_dim.31
  44.0 3.9 %all-to-all-start.1 = ((f32[32,2,8,512]{3,2,1,0:T(8,128)}), f32[32,2,8,512]{3,2,1,0:T(8,128)S(1)}, u32[]{:S(2)}, u32[]{:S(2)}) async-start(f32[32,2,8,512]{3,2,1,0:T(8,128)} %broadcast_in_dim.31), calls=%async_computation.1 | async-start | bytes 2097152 | tf_op jit(solution)/shard_map/all_to_all | solution.py:355
  48.0 0.0 all-gather.5.cloned.1.call-start
  48.0 1.6 collective-permute-start
  49.6 21.0 %collective-permute-done.refs_0_ = f32[32,6656]{1,0:T(8,128)S(1)} collective-permute-done((f32[32,6656]{1,0:T(8,128)}, f32[32,6656]{1,0:T(8,128)S(1)}, u32[]{:S(2)}, u32[]{:S(2)}) %collective-permute-start) | collective-permute-done | bytes 852000 | tf_op jit(solution)/shard_map/ppermute | solution.py:24
  70.5 0.0 all-to-all-done.1.a00
  70.5 0.3 collective-permute-start.1
  70.8 22.2 %pivot_block_0.1 = (f32[512,512]{1,0:T(8,128)S(1)}, f32[1,512]{1,0:T(1,128)S(1)}, f32[256,1536]{1,0:T(8,128)}, bf16[256,512]{1,0:T(8,128)(2,1)S(1)}) custom-call(s32[1]{0:T(128)} %bitcast.row_ref, f32[32,2,8,512]{3,2,1,0:T(8,128)S(1)} %all-to-all-done.1.a00, f32[1,256,8192]{2,1,0:T(8,128)} %panel.5), custom_call_target="tpu_custom_call" | custom-call | flops 20000000000 | bytes 4000000 | tf_op jit(solution)/shard_map/pivot_block_0/pallas_call | solution.py:213
  93.0 0.0 copy-done.5
  93.0 1.0 copy-done.15
  94.1 0.0 collective-permute-done.1.refs_1_
  94.1 0.9 copy-done.7
  95.0 1.4 collective-permute-start.2
  96.5 7.3 %collective-permute-done.2.own = bf16[256,512]{1,0:T(8,128)(2,1)S(1)} collective-permute-done((bf16[256,512]{1,0:T(8,128)(2,1)S(1)}, bf16[256,512]{1,0:T(8,128)(2,1)S(1)}, u32[]{:S(2)}, u32[]{:S(2)}) %collective-permute-start.2) | collective-permute-done | bytes 262176 | tf_op jit(solution)/shard_map/ppermute | solution.py:24
  103.8 0.7 copy-done.3
  104.5 0.0 all-gather.5.cloned.1.call-update
  104.5 0.0 all-gather.7.cloned.1.call-start
  104.6 0.3 collective-permute-start.3
  104.9 0.0 copy-start.16
  104.9 1.2 copy-done.16
  106.1 25.3 %pivot_block_1.1 = (f32[512,512]{1,0:T(8,128)S(1)}, f32[1,512]{1,0:T(1,128)S(1)}, f32[256,1536]{1,0:T(8,128)}, bf16[256,512]{1,0:T(8,128)(2,1)S(1)}, bf16[512,512]{1,0:T(8,128)(2,1)S(1)}) custom-call(s32[1]{0:T(128)} %bitcast.row_ref, f32[32,4,8,1536]{3,2,1,0:T(8,128)} %bitcast.12, f32[32,4,8,1536]{3,2,1,0:T(8,128)} %bitcast.13, ...), custom_call_target="tpu_custom_call", output_to_operand_aliasing={{2}: (6, {})} | custom-call | flops 20000000000 | bytes 4000000 | tf_op jit(solution)/shard_map/pivot_block_1/pallas_call | solution.py:213
  131.4 0.7 copy-done.13
  132.2 0.0 collective-permute-done.3.refs_2_
  132.2 1.1 collective-permute-start.5
  133.3 0.0 copy-done.10
  133.3 1.7 collective-permute-start.6
  135.0 1.0 copy-done.14
  136.0 27.9 %pivot_block_2.1 = (f32[1,512]{1,0:T(1,128)S(1)}, f32[256,1536]{1,0:T(8,128)}, bf16[256,512]{1,0:T(8,128)(2,1)S(1)}) custom-call(s32[1]{0:T(128)} %bitcast.row_ref, f32[32,4,8,1536]{3,2,1,0:T(8,128)} %bitcast.14, f32[32,4,8,1536]{3,2,1,0:T(8,128)} %bitcast.15, f32[32,4,8,1536]{3,2,1,0:T(8,128)} %bitcast.16, ...), custom_call_target="tpu_custom_call", output_to_operand_aliasing={{1}: (10, {})} | custom-call | flops 20000000000 | bytes 4000000 | tf_op jit(solution)/shard_map/pivot_block_2/pallas_call | solution.py:213
  163.9 0.0 collective-permute-done.5
  163.9 3.5 %collective-permute-done.6.refs_3_ = f32[48,6656]{1,0:T(8,128)S(1)} collective-permute-done((f32[48,6656]{1,0:T(8,128)S(1)}, f32[48,6656]{1,0:T(8,128)S(1)}, u32[]{:S(2)}, u32[]{:S(2)}) %collective-permute-start.6) | collective-permute-done | bytes 1277984 | tf_op jit(solution)/shard_map/ppermute | solution.py:24
  167.4 0.0 collective-permute-start.7
  167.5 7.6 %collective-permute-done.7 = bf16[256,512]{1,0:T(8,128)(2,1)S(1)} collective-permute-done((bf16[256,512]{1,0:T(8,128)(2,1)S(1)}, bf16[256,512]{1,0:T(8,128)(2,1)S(1)}, u32[]{:S(2)}, u32[]{:S(2)}) %collective-permute-start.7) | collective-permute-done | bytes 262176 | tf_op jit(solution)/shard_map/ppermute | solution.py:24
  175.0 0.0 copy-start.1
  175.1 0.8 copy-done.1
  175.9 0.0 all-gather.7.cloned.1.call-update
  175.9 0.3 collective-permute-start.8
  176.9 0.1 pad_add_fusion
  177.0 0.3 collective-permute-start.4
  177.2 58.8 %collective-permute-done.4 = s32[53]{0:T(128)S(1)} collective-permute-done((s32[53]{0:T(128)S(1)}, s32[53]{0:T(128)S(1)}, u32[]{:S(2)}, u32[]{:S(2)}) %collective-permute-start.4) | collective-permute-done | bytes 244 | tf_op jit(solution)/shard_map/ppermute | solution.py:24
  236.1 0.6 slice.23
  236.7 0.7 pad_add_fusion.1.info_ref
  237.4 0.0 collective-permute-done.8.refs_4_
  237.4 1.4 copy-done.6
  238.8 1.2 copy-done.8
  239.9 12.4 %transposed_base.1.base = f32[6656,256]{1,0:T(8,128)} custom-call(bf16[8192,512]{1,0:T(8,128)(2,1)} %all-gather.5.cloned.1.call-done.w, bf16[256,512]{1,0:T(8,128)(2,1)S(1)} %copy-done.4, f32[32,6656]{1,0:T(8,128)S(1)} %copy-done.6, f32[32,6656]{1,0:T(8,128)S(1)} %copy-done.8, f32[40,6656]{1,0:T(8,128)S(1)} %collective-permute-done.3.refs_2_, ...), custom_call_target="tpu_custom_call" | custom-call | tf_op jit(solution)/shard_map/transposed_base/pallas_call | solution.py:262
  252.3 14.6 %contributions.1 = bf16[32,256,256]{2,1,0:T(8,128)(2,1)S(1)} custom-call(s32[52]{0:T(128)S(1)} %bitcast.9, s32[2]{0:T(128)S(1)} %pad_add_fusion.1.info_ref, f32[6656,256]{1,0:T(8,128)} %transposed_base.1.base, bf16[8192,1024]{1,0:T(8,128)(2,1)} %all-gather.7.cloned.1.call-done.w, bf16[256,1024]{1,0:T(8,128)(2,1)S(1)} %copy-done.2), custom_call_target="tpu_custom_call" | custom-call | tf_op jit(solution)/shard_map/contributions/pallas_call | solution.py:301
  266.9 0.0 copy-start
  266.9 2.0 copy-done
  268.9 7.4 %all-to-all-start.2 = ((bf16[32,256,256]{2,1,0:T(8,128)(2,1)}), bf16[32,256,256]{2,1,0:T(8,128)(2,1)}, u32[]{:S(2)}, u32[]{:S(2)}) async-start(bf16[32,256,256]{2,1,0:T(8,128)(2,1)} %copy-done), calls=%async_computation.2 | async-start | bytes 8388608 | tf_op jit(solution)/shard_map/all_to_all | solution.py:355
  276.4 0.6 iota_compare_fusion.1
  277.0 0.1 select_reduce_fusion
  277.1 0.6 maximum_multiply_fusion
  277.7 52.1 %all-to-all-done.2.refs_0_.refs_1_.refs_2_.refs_3_.refs_4_.refs_5_.refs_6_.refs_7_ = bf16[32,256,256]{2,1,0:T(8,128)(2,1)} async-done(((bf16[32,256,256]{2,1,0:T(8,128)(2,1)}), bf16[32,256,256]{2,1,0:T(8,128)(2,1)}, u32[]{:S(2)}, u32[]{:S(2)}) %all-to-all-start.2) | async-done | bytes 4194336 | tf_op jit(solution)/shard_map/all_to_all | solution.py:355
  329.8 7.5 %parent_rows.1 = bf16[256,8192]{1,0:T(8,128)(2,1)} custom-call(s32[64]{0:T(128)S(1)} %compare_select_fusion.source_ref, bf16[32,256,256]{2,1,0:T(8,128)(2,1)} %all-to-all-done.2.refs_0_.refs_1_.refs_2_.refs_3_.refs_4_.refs_5_.refs_6_.refs_7_, bf16[32,256,256]{2,1,0:T(8,128)(2,1)} %all-to-all-done.2.refs_0_.refs_1_.refs_2_.refs_3_.refs_4_.refs_5_.refs_6_.refs_7_, ...), custom_call_target="tpu_custom_call" | custom-call | tf_op jit(solution)/shard_map/parent_rows/pallas_call | solution.py:340
  (27 shorter events, 0.1 us)
Async XLA Ops:
  9.8 32.4 %all-to-all-start = ((f32[32,8,1536]{2,1,0:T(8,128)}), f32[32,8,1536]{2,1,0:T(8,128)S(1)}, u32[]{:S(2)}, u32[]{:S(2)}) async-start(f32[32,8,1536]{2,1,0:T(8,128)} %slice_bitcast_fusion), calls=%async_computation | async-start | bytes 3145728 | tf_op jit(solution)/shard_map/all_to_all | solution.py:355
  18.2 86.6 %all-gather.9.cloned.1.call-start = ((), (), s32[]{:S(2)}) async-start(), calls=%async_computation.5 | async-start | bytes 6488064 | tf_op jit(solution)/shard_map/all_gather | solution.py:371
  27.6 1.0 copy-start.9
  28.6 0.9 copy-start.11
  29.5 1.0 copy-start.12
  44.0 26.5 %all-to-all-start.1 = ((f32[32,2,8,512]{3,2,1,0:T(8,128)}), f32[32,2,8,512]{3,2,1,0:T(8,128)S(1)}, u32[]{:S(2)}, u32[]{:S(2)}) async-start(f32[32,2,8,512]{3,2,1,0:T(8,128)} %broadcast_in_dim.31), calls=%async_computation.1 | async-start | bytes 2097152 | tf_op jit(solution)/shard_map/all_to_all | solution.py:355
  48.0 189.4 %all-gather.5.cloned.1.call-start = ((), (), s32[]{:S(2)}) async-start(), calls=%async_computation.3 | async-start | bytes 8650752 | tf_op jit(solution)/shard_map/all_gather | solution.py:386
  48.0 22.5 %collective-permute-start = (f32[32,6656]{1,0:T(8,128)}, f32[32,6656]{1,0:T(8,128)S(1)}, u32[]{:S(2)}, u32[]{:S(2)}) collective-permute-start(f32[32,6656]{1,0:T(8,128)} %copy-done.12), channel_id=1, source_target_pairs={{0,32},{32,64},{64,96},{96,0},{1,33},{33,65},{65,97},{97,1},{2,34}... | collective-permute-start | bytes 2555912 | tf_op jit(solution)/shard_map/ppermute | solution.py:24
  70.5 22.5 %copy-start.5 = (f32[32,6656]{1,0:T(8,128)}, f32[32,6656]{1,0:T(8,128)S(1)}, u32[]{:S(2)}) copy-start(f32[32,6656]{1,0:T(8,128)S(1)} %collective-permute-done.refs_0_) | copy-start | bytes 2555908
  70.5 23.6 %collective-permute-start.1 = (f32[32,6656]{1,0:T(8,128)}, f32[32,6656]{1,0:T(8,128)S(1)}, u32[]{:S(2)}, u32[]{:S(2)}) collective-permute-start(f32[32,6656]{1,0:T(8,128)} %copy-done.11), channel_id=1, source_target_pairs={{0,32},{32,64},{64,96},{96,0},{1,33},{33,65},{65,97},{97,1},{2,34}... | collective-permute-start | bytes 2555912 | tf_op jit(solution)/shard_map/ppermute | solution.py:24
  93.0 1.0 copy-start.15
  94.1 0.9 copy-start.7
  95.0 8.8 %collective-permute-start.2 = (bf16[256,512]{1,0:T(8,128)(2,1)S(1)}, bf16[256,512]{1,0:T(8,128)(2,1)S(1)}, u32[]{:S(2)}, u32[]{:S(2)}) collective-permute-start(bf16[256,512]{1,0:T(8,128)(2,1)S(1)} %get-tuple-element.84.wb0), channel_id=1, source_target_pairs={{0,32},{32,64},{64,96},{96,0},{1,33},{33,65},{65,97},{97,1},{2,34}... | collective-permute-start | bytes 786440 | tf_op jit(solution)/shard_map/ppermute | solution.py:24
  103.8 0.7 copy-start.3
  104.5 147.8 %all-gather.7.cloned.1.call-start = ((), (), s32[]{:S(2)}) async-start(), calls=%async_computation.4 | async-start | bytes 17301504 | tf_op jit(solution)/shard_map/all_gather | solution.py:403
  104.6 27.6 %collective-permute-start.3 = (f32[40,6656]{1,0:T(8,128)S(1)}, f32[40,6656]{1,0:T(8,128)S(1)}, u32[]{:S(2)}, u32[]{:S(2)}) collective-permute-start(f32[40,6656]{1,0:T(8,128)S(1)} %get-tuple-element.96), channel_id=1, source_target_pairs={{0,32},{32,64},{64,96},{96,0},{1,33},{33,65},{65,97},{97,1},{2,34}... | collective-permute-start | bytes 3194888 | tf_op jit(solution)/shard_map/ppermute | solution.py:24
  104.9 1.2 copy-start.16
  106.1 27.2 %copy-start.10 = (f32[48,6656]{1,0:T(8,128)S(1)}, f32[48,6656]{1,0:T(8,128)}, u32[]{:S(2)}) copy-start(f32[48,6656]{1,0:T(8,128)} %copy-done.9) | copy-start | bytes 3833860
  131.4 0.7 copy-start.13
  132.2 31.7 %collective-permute-start.5 = (bf16[256,512]{1,0:T(8,128)(2,1)S(1)}, bf16[256,512]{1,0:T(8,128)(2,1)S(1)}, u32[]{:S(2)}, u32[]{:S(2)}) collective-permute-start(bf16[256,512]{1,0:T(8,128)(2,1)S(1)} %get-tuple-element.101.wb1), channel_id=1, source_target_pairs={{0,32},{32,64},{64,96},{96,0},{1,33},{33,65},{65,97},{97,1},{2,34}... | collective-permute-start | bytes 786440 | tf_op jit(solution)/shard_map/ppermute | solution.py:24
  133.3 34.2 %collective-permute-start.6 = (f32[48,6656]{1,0:T(8,128)S(1)}, f32[48,6656]{1,0:T(8,128)S(1)}, u32[]{:S(2)}, u32[]{:S(2)}) collective-permute-start(f32[48,6656]{1,0:T(8,128)S(1)} %copy-done.10), channel_id=1, source_target_pairs={{0,32},{32,64},{64,96},{96,0},{1,33},{33,65},{65,97},{97,1},{2,34}... | collective-permute-start | bytes 3833864 | tf_op jit(solution)/shard_map/ppermute | solution.py:24
  135.0 1.0 copy-start.14
  136.0 40.8 %copy-start.17 = (s32[1,52]{1,0:T(1,128)S(1)}, s32[1,52]{1,0:T(1,128)}, u32[]{:S(2)}) copy-start(s32[1,52]{1,0:T(1,128)} %param.4) | copy-start | bytes 628
  136.0 101.4 %copy-start.4 = (bf16[256,512]{1,0:T(8,128)(2,1)S(1)}, bf16[256,512]{1,0:T(8,128)(2,1)}, u32[]{:S(2)}) copy-start(bf16[256,512]{1,0:T(8,128)(2,1)} %copy-done.3) | copy-start | bytes 786436
  167.4 7.6 %collective-permute-start.7 = (bf16[256,512]{1,0:T(8,128)(2,1)S(1)}, bf16[256,512]{1,0:T(8,128)(2,1)S(1)}, u32[]{:S(2)}, u32[]{:S(2)}) collective-permute-start(bf16[256,512]{1,0:T(8,128)(2,1)S(1)} %get-tuple-element.114), channel_id=1, source_target_pairs={{0,32},{32,64},{64,96},{96,0},{1,33},{33,65},{65,97},{97,1},{2,34}... | collective-permute-start | bytes 786440 | tf_op jit(solution)/shard_map/ppermute | solution.py:24
  175.0 0.8 copy-start.1
  175.9 61.5 %collective-permute-start.8 = (f32[104,6656]{1,0:T(8,128)}, f32[104,6656]{1,0:T(8,128)}, u32[]{:S(2)}, u32[]{:S(2)}) collective-permute-start(f32[104,6656]{1,0:T(8,128)} %get-tuple-element.124), channel_id=1, source_target_pairs={{0,32},{32,64},{64,96},{96,0},{1,33},{33,65},{65,97},{97,1},{2,34}... | collective-permute-start | bytes 8306696 | tf_op jit(solution)/shard_map/ppermute | solution.py:24
  177.0 59.1 %collective-permute-start.4 = (s32[53]{0:T(128)S(1)}, s32[53]{0:T(128)S(1)}, u32[]{:S(2)}, u32[]{:S(2)}) collective-permute-start(s32[53]{0:T(128)S(1)} %pad_add_fusion), channel_id=1, source_target_pairs={{0,32},{32,64},{64,96},{96,0},{1,33},{33,65},{65,97},{97,1},{2,34}... | collective-permute-start | bytes 644 | tf_op jit(solution)/shard_map/ppermute | solution.py:24
  237.4 14.9 %copy-start.2 = (bf16[256,1024]{1,0:T(8,128)(2,1)S(1)}, bf16[256,1024]{1,0:T(8,128)(2,1)}, u32[]{:S(2)}) copy-start(bf16[256,1024]{1,0:T(8,128)(2,1)} %copy-done.1) | copy-start | bytes 1572868
  237.4 1.4 copy-start.6
  238.8 1.2 copy-start.8
  266.9 2.0 copy-start
  268.9 60.9 %all-to-all-start.2 = ((bf16[32,256,256]{2,1,0:T(8,128)(2,1)}), bf16[32,256,256]{2,1,0:T(8,128)(2,1)}, u32[]{:S(2)}, u32[]{:S(2)}) async-start(bf16[32,256,256]{2,1,0:T(8,128)(2,1)} %copy-done), calls=%async_computation.2 | async-start | bytes 8388608 | tf_op jit(solution)/shard_map/all_to_all | solution.py:355
Sparse Core Ops, SparseCore 0:
  43.0 52.6 all-gather.8
  104.6 52.8 all-gather.4
  176.0 71.5 all-gather.6

commit v3 on v2

--- a/solution.py
+++ b/solution.py
@@ -15,7 +15,8 @@
 PT = 64
 SKIP = NPIV // TILE
 VMEM_LIMIT = 48 << 20
-CHUNKS = (32, 32, 40, 48, 104)
+VMEM_MOST = 62 << 20
+CHUNKS = (24, 32, 32, 80, 88)
 HIGHEST = lax.Precision.HIGHEST
 
 
@@ -36,7 +37,7 @@
     )
 
 
-def leaf_inverse(strips):
+def leaf_inverse(strips, corner_ref):
     lanes = lax.broadcasted_iota(jnp.int32, (8, TILE), 1)
     subs = lax.broadcasted_iota(jnp.int32, (8, TILE), 0)
     count = len(strips)
@@ -54,8 +55,12 @@
     for s in range(count):
         k = 8 * s
         last = s + 1 == count
-        b = [lane_splat(t[s], k + j) for j in range(8)]
-        corner = [[row_splat(b[j], i) for j in range(i + 1)] for i in range(8)]
+        corner = [[None] * 8 for _ in range(8)]
+        for j in range(8):
+            slot = s % 2 * 8 + j
+            corner_ref[slot] = lane_splat(t[s], k + j)
+            for i in range(j, 8):
+                corner[i][j] = row_splat(corner_ref[slot], i)
         rt = None if last else [row_splat(t[s], i) for i in range(8)]
         re = [row_splat(e[s], i) for i in range(8)]
         l = [[None] * 8 for _ in range(8)]
@@ -91,16 +96,16 @@
     return out, diag[0:1, :]
 
 
-def block_inverse(a_ref, x_ref, diag_ref, leaf_ref):
+def block_inverse(ax_ref, diag_ref, leaf_ref, corner_ref):
     steps = PB // TILE
-    x_ref[...] = jnp.zeros_like(x_ref)
+    ax_ref[:, PB : 2 * PB] = jnp.zeros((PB, PB), jnp.float32)
 
     def step(j, carry):
         o = pl.multiple_of(j * TILE, TILE)
         strips = [
-            a_ref[pl.ds(pl.multiple_of(o + 8 * r, 8), 8), pl.ds(o, TILE)] for r in range(TILE // 8)
+            ax_ref[pl.ds(pl.multiple_of(o + 8 * r, 8), 8), pl.ds(o, TILE)] for r in range(TILE // 8)
         ]
-        rows, diag = leaf_inverse(strips)
+        rows, diag = leaf_inverse(strips, corner_ref)
         for r in range(TILE // 8):
             leaf_ref[8 * r : 8 * r + 8, :] = rows[r]
         diag_ref[:, pl.ds(o, TILE)] = diag
@@ -110,118 +115,90 @@
             def _():
                 lo, hi = q * TILE, (q + 1) * TILE
                 leaf = leaf_ref[...]
-                x_ref[lo:hi, lo:hi] = leaf
-                if q:
-                    x_ref[lo:hi, 0:lo] = dot_nn(leaf, x_ref[lo:hi, 0:lo], HIGHEST)
+                row = dot_nn(leaf, ax_ref[lo:hi, hi : PB + lo], HIGHEST)
+                ax_ref[lo:hi, hi : PB + lo] = row
+                ax_ref[lo:hi, PB + lo : PB + hi] = leaf
                 if q + 1 < steps:
-                    p = dot_nt(a_ref[hi:PB, lo:hi], leaf, HIGHEST)
-                    for b in range(q + 1, steps):
-                        pb = p[(b - q - 1) * TILE :]
-                        a_ref[b * TILE : PB, b * TILE : (b + 1) * TILE] -= dot_nt(pb, pb[0:TILE], HIGHEST)
-                    x_ref[hi:PB, 0:hi] -= dot_nn(p, x_ref[lo:hi, 0:hi], HIGHEST)
+                    column = dot_nt(ax_ref[hi:PB, lo:hi], leaf, HIGHEST)
+                    row = jnp.concatenate([row, leaf], axis=1)
+                    ax_ref[hi:PB, hi : PB + hi] -= dot_nn(column, row, HIGHEST)
 
         return carry
 
     lax.fori_loop(0, steps, step, 0)
 
 
-def finish_panel(k, first_row, panel, inv, diag, factor_ref, wb_ref):
+def finish_panel(k, first_row, panel, inv, diag):
     w = dot_nt(panel, inv, HIGHEST)
     rows = lax.broadcasted_iota(jnp.int32, w.shape, 0) + first_row
     w = jnp.where(rows >= k * PB, w, 0.0)
-    factor_ref[...] = w * (1.0 / diag)
-    wb_ref[...] = w.astype(jnp.bfloat16)
-
-
-def lead(ref):
-    return ref[...].reshape(PB, PB)
-
-
-def kernel_0(row_ref, a00, panel, inv_ref, diag_ref, factor_ref, wb_ref, a_ref, leaf_ref):
-    for s in range(2):
-        a_ref[s * 256 : (s + 1) * 256, :] = a00[:, s].reshape(256, PB)
-    block_inverse(a_ref, inv_ref, diag_ref, leaf_ref)
-    finish_panel(0, row_ref[0], panel[0], inv_ref[...], diag_ref[...], factor_ref, wb_ref)
+    return w.astype(jnp.bfloat16), w * (1.0 / diag)
 
 
 def put_block(ref):
     return jnp.concatenate([ref[:, s].reshape(256, PB) for s in range(2)], axis=0)
 
 
-def kernel_1(
-    row_ref, a10, a11, panel, inv0, wb0, factor_in, inv_ref, diag_ref, factor_ref, wb_ref, lb10_ref, a_ref, leaf_ref
+def kernel_0(row_ref, a00, panel, inv_ref, diag_ref, factor_ref, wb_ref, ax_ref, leaf_ref, corner_ref):
+    ax_ref[:, 0:PB] = put_block(a00)
+    block_inverse(ax_ref, diag_ref, leaf_ref, corner_ref)
+    inv = ax_ref[:, PB : 2 * PB]
+    inv_ref[...] = inv
+    wb_ref[...], factor_ref[...] = finish_panel(0, row_ref[0], panel[0], inv, diag_ref[...])
+
+
+def kernel_12(
+    row_ref, a02, a10, a11, a21, a22, p1, p2, inv0, wb0, diag1_ref, diag2_ref, factor_ref, wb_ref, ax_ref, leaf_ref,
+    corner_ref, lb20_ref, lb21_ref, a21_ref, a22_ref, p2_ref
 ):
     lb10 = dot_nt(put_block(a10), inv0[...], HIGHEST).astype(jnp.bfloat16)
-    lb10_ref[...] = lb10
-    a_ref[...] = put_block(a11) - dot_nt(lb10, lb10)
-    block_inverse(a_ref, inv_ref, diag_ref, leaf_ref)
-    mine = panel[0] - dot_nt(wb0[...], lb10_ref[...])
-    finish_panel(1, row_ref[0], mine, inv_ref[...], diag_ref[...], factor_ref, wb_ref)
-
-
-def kernel_2(
-    row_ref, a20, a21, a22, panel, inv0, inv1, lb10, wb0, wb1, factor_in, diag_ref, factor_ref, wb_ref, a_ref, leaf_ref,
-    inv_ref, lb20_ref, lb21_ref
-):
-    lb20 = dot_nt(put_block(a20), inv0[...], HIGHEST).astype(jnp.bfloat16)
-    lb20_ref[...] = lb20
-    lb21 = dot_nt(put_block(a21) - dot_nt(lb20, lb10[...]), inv1[...], HIGHEST).astype(jnp.bfloat16)
+    lb20_ref[...] = dot_nn(inv0[...], put_block(a02), HIGHEST).T.astype(jnp.bfloat16)
+    ax_ref[:, 0:PB] = put_block(a11) - dot_nt(lb10, lb10)
+    a21_ref[...] = put_block(a21) - dot_nt(lb20_ref[...], lb10)
+    a22_ref[...] = put_block(a22) - dot_nt(lb20_ref[...], lb20_ref[...])
+    mine = p1[0] - dot_nt(wb0[...], lb10)
+    p2_ref[...] = p2[0] - dot_nt(wb0[...], lb20_ref[...])
+    block_inverse(ax_ref, diag1_ref, leaf_ref, corner_ref)
+    inv = ax_ref[:, PB : 2 * PB]
+    lb21 = dot_nt(a21_ref[...], inv, HIGHEST).astype(jnp.bfloat16)
     lb21_ref[...] = lb21
-    a_ref[...] = put_block(a22) - dot_nt(lb20, lb20) - dot_nt(lb21, lb21)
-    block_inverse(a_ref, inv_ref, diag_ref, leaf_ref)
-    mine = panel[0] - dot_nt(wb0[...], lb20_ref[...]) - dot_nt(wb1[...], lb21_ref[...])
-    finish_panel(2, row_ref[0], mine, inv_ref[...], diag_ref[...], factor_ref, wb_ref)
+    wb, factor = finish_panel(1, row_ref[0], mine, inv, diag1_ref[...])
+    wb_ref[:, 0:PB], factor_ref[:, 0:PB] = wb, factor
+    ax_ref[:, 0:PB] = a22_ref[...] - dot_nt(lb21, lb21)
+    block_inverse(ax_ref, diag2_ref, leaf_ref, corner_ref)
+    mine = p2_ref[...] - dot_nt(wb_ref[:, 0:PB], lb21_ref[...])
+    wb, factor = finish_panel(2, row_ref[0], mine, ax_ref[:, PB : 2 * PB], diag2_ref[...])
+    wb_ref[:, PB : 2 * PB], factor_ref[:, PB : 2 * PB] = wb, factor
 
 
 def whole(shape):
     return pl.BlockSpec(shape, lambda i: (0,) * len(shape))
 
 
-def factor_step(k, first_row, front, leading, carried, factor):
-    rows = front.shape[1]
-    specs = [pl.BlockSpec(memory_space=pltpu.SMEM)]
-    args = [first_row]
-    for array, i, j in leading:
-        specs.append(pl.BlockSpec((array.shape[0], 2, 8, PB), lambda _, i=i, j=j: (0, i, 0, j)))
-        args.append(array)
-    specs.append(pl.BlockSpec((1, rows, PB), lambda _: (0, 0, k)))
-    args.append(front)
-    for array in carried:
-        specs.append(whole(array.shape))
-        args.append(array)
+def factor_step(blocks, first_row, args, specs, rows):
+    first = blocks[0] == 0
+    width = len(blocks) * PB
+    outs = [jax.ShapeDtypeStruct((1, PB), jnp.float32) for _ in blocks]
+    outs += [jax.ShapeDtypeStruct((rows, width), jnp.float32), jax.ShapeDtypeStruct((rows, width), jnp.bfloat16)]
     square = jax.ShapeDtypeStruct((PB, PB), jnp.float32)
-    diag = jax.ShapeDtypeStruct((1, PB), jnp.float32)
-    factors = jax.ShapeDtypeStruct((rows, NPIV), jnp.float32)
-    wb = jax.ShapeDtypeStruct((rows, PB), jnp.bfloat16)
-    factor_spec = pl.BlockSpec((rows, PB), lambda _: (0, k))
-    outs = [diag, factors, wb]
-    out_specs = [whole(diag.shape), factor_spec, whole(wb.shape)]
-    scratch = [pltpu.VMEM((PB, PB), jnp.float32), pltpu.VMEM((TILE, TILE), jnp.float32)]
-    if k < 2:
+    scratch = [pltpu.VMEM((PB, 2 * PB), jnp.float32), pltpu.VMEM((TILE, TILE), jnp.float32)]
+    scratch.append(pltpu.VMEM((16, 8, TILE), jnp.float32))
+    if first:
         outs.insert(0, square)
-        out_specs.insert(0, whole(square.shape))
     else:
-        scratch += [pltpu.VMEM((PB, PB), jnp.float32)] + [pltpu.VMEM((PB, PB), jnp.bfloat16)] * 2
-    if k == 1:
-        outs.append(jax.ShapeDtypeStruct((PB, PB), jnp.bfloat16))
-        out_specs.append(whole((PB, PB)))
-    aliases = {}
-    if k:
-        specs.append(pl.BlockSpec(memory_space=pl.ANY))
-        args.append(factor)
-        aliases = {len(args) - 1: 2 if k == 1 else 1}
+        scratch += [pltpu.VMEM((PB, PB), jnp.bfloat16)] * 2 + [pltpu.VMEM((PB, PB), jnp.float32)] * 2
+        scratch.append(pltpu.VMEM((rows, PB), jnp.float32))
     return pl.pallas_call(
-        (kernel_0, kernel_1, kernel_2)[k],
+        kernel_0 if first else kernel_12,
         grid=(1,),
-        in_specs=specs,
-        out_specs=out_specs,
+        in_specs=[pl.BlockSpec(memory_space=pltpu.SMEM), *specs],
+        out_specs=[whole(x.shape) for x in outs],
         out_shape=outs,
         scratch_shapes=scratch,
-        input_output_aliases=aliases,
-        compiler_params=pltpu.CompilerParams(vmem_limit_bytes=VMEM_LIMIT),
-        cost_estimate=pl.CostEstimate(flops=20_000_000_000, bytes_accessed=4_000_000, transcendentals=0),
-        name=f"pivot_block_{k}",
-    )(*args)
+        compiler_params=pltpu.CompilerParams(vmem_limit_bytes=VMEM_LIMIT if first else VMEM_MOST),
+        cost_estimate=pl.CostEstimate(flops=20_000_000_000 * len(blocks), bytes_accessed=4_000_000, transcendentals=0),
+        name=f"pivot_block_{blocks[0]}",
+    )(first_row, *args)
 
 
 def cut_kernel(front, *outs):
@@ -239,7 +216,7 @@
         grid=(width // PB,),
         in_specs=[pl.BlockSpec((1, rows, PB), lambda i: (0, 0, NPB + i))],
         out_specs=[pl.BlockSpec((c, PB), lambda i: (0, i)) for c in chunks],
-        out_shape=[jax.ShapeDtypeStruct((c, width), jnp.float32) for c in chunks],
+        out_shape=[pltpu.HBM((c, width), jnp.float32) for c in chunks],
         compiler_params=pltpu.CompilerParams(vmem_limit_bytes=VMEM_LIMIT),
         name="cut_rows",
     )(front)
@@ -286,13 +263,11 @@
     value = base[...] - dot_nn(w[...], own_ref[...])
     count = value.shape[0] // TILE
     for n in range(count):
-
-        @pl.when(count * i + n < info_ref[1])
-        def _():
-            target = target_ref[count * i + n]
-            at = pl.multiple_of(target % 2 * TILE, TILE)
-            tile = jnp.where(keep, value[n * TILE : (n + 1) * TILE], 0.0)
-            out_ref[target // 2, pl.ds(at, TILE), :] = tile.astype(jnp.bfloat16)
+        target = target_ref[count * i + n]
+        live = count * i + n < info_ref[1]
+        at = pl.multiple_of(target % 2 * TILE, TILE)
+        tile = jnp.where(keep & live, value[n * TILE : (n + 1) * TILE], 0.0)
+        out_ref[target // 2, pl.ds(at, TILE), :] = tile.astype(jnp.bfloat16)
 
 
 def contributions(targets, info, base, own, gathered):
@@ -311,7 +286,7 @@
             out_specs=pl.BlockSpec((PT // 2, 2 * TILE, rows), lambda i, target, info: (0, 0, 0)),
             scratch_shapes=[pltpu.VMEM((depth, rows), jnp.bfloat16)],
         ),
-        out_shape=jax.ShapeDtypeStruct((PT // 2, 2 * TILE, rows), jnp.bfloat16),
+        out_shape=pltpu.HBM((PT // 2, 2 * TILE, rows), jnp.bfloat16),
         compiler_params=pltpu.CompilerParams(vmem_limit_bytes=VMEM_LIMIT),
         name="contributions",
     )(targets, info, base, gathered, own)
@@ -362,13 +337,16 @@
     first_row = (helper * rows).astype(jnp.int32).reshape(1)
     piece = rows // helpers
 
-    chunks = cut(front, CHUNKS)
-
-    panel = front[0, :, :NPIV]
-    scattered = exchange(panel.reshape(helpers, piece, NPIV))[: NPIV // rows]
+    chunks = list(cut(front, CHUNKS))
+
+    pair = helper // (PB // rows)
+    first = jnp.where(pair == 2, 1, 0) * PB
+    second = jnp.where(pair == 1, 1, 2) * PB
+    panel = jnp.concatenate([lax.dynamic_slice(front[0], (0, c), (rows, PB)) for c in (first, second)], axis=1)
+    scattered = exchange(panel.reshape(helpers, piece, 2 * PB))[: NPIV // rows]
     scattered, *chunks = lax.optimization_barrier((scattered, *chunks))
     block_0 = exchange(jnp.broadcast_to(scattered[None, :2, :, :PB], (helpers, 2, piece, PB)))
-    rest = lax.all_gather(scattered[2:], "helper", axis=0)
+    rest = lax.all_gather(scattered, "helper", axis=0)
     chunks[0] = shifted(chunks[0], "front", 1)
 
     tiling = shifted(jnp.concatenate([tile_map[0], live_tiles]), "front", 1)
@@ -377,36 +355,39 @@
     info = jnp.concatenate([first_row, live_count.reshape(1)])
 
     block_0, *chunks = lax.optimization_barrier((block_0, *chunks))
-    inv0, diag0, factor, wb0 = factor_step(0, first_row, front, [(block_0, 0, 0)], [], None)
+    panel_0 = pl.BlockSpec((1, rows, PB), lambda _: (0, 0, 0))
+    specs = [whole(block_0.shape), panel_0]
+    inv0, diag0, factor0, wb0 = factor_step((0,), first_row, [block_0, front], specs, rows)
     chunks[1] = shifted(chunks[1], "front", 1)
+    chunks[2] = shifted(chunks[2], "front", -1)
 
     wb0, *chunks = lax.optimization_barrier((wb0, *chunks))
     own0 = shifted(wb0, "front", 1)
     inv0, own0, *chunks = lax.optimization_barrier((inv0, own0, *chunks))
     all0 = lax.all_gather(own0, "helper", axis=0, tiled=True)
-    inv1, diag1, factor, wb1, lb10 = factor_step(
-        1, first_row, front, [(rest, 0, 0), (rest, 0, 1)], [inv0, wb0], factor
-    )
-    chunks[2] = shifted(chunks[2], "front", 1)
-
-    inv1, wb1, *chunks = lax.optimization_barrier((inv1, wb1, *chunks))
-    diag2, factor, wb2 = factor_step(
-        2, first_row, front, [(rest, 1, 0), (rest, 1, 1), (rest, 1, 2)], [inv0, inv1, lb10, wb0, wb1], factor
-    )
-    own1 = shifted(wb1, "front", 1)
+    specs = [
+        pl.BlockSpec((helpers, 2, piece, PB), lambda _, i=i, j=j: (0, i, 0, j))
+        for i, j in [(0, 1), (1, 0), (1, 1), (2, 0), (2, 1)]
+    ]
+    specs += [pl.BlockSpec((1, rows, PB), lambda _, k=k: (0, 0, k)) for k in (1, 2)]
+    specs += [whole(inv0.shape), whole(wb0.shape)]
+    args = [rest] * 5 + [front] * 2 + [inv0, wb0]
+    diag1, diag2, factor12, wb12 = factor_step((1, 2), first_row, args, specs, rows)
     chunks[3] = shifted(chunks[3], "front", 1)
-
-    wb2, own1, *chunks = lax.optimization_barrier((wb2, own1, *chunks))
-    own2 = shifted(wb2, "front", 1)
-    own2, *chunks = lax.optimization_barrier((own2, *chunks))
-    own12 = jnp.concatenate([own1, own2], axis=1)
+    chunks[2] = shifted(chunks[2], "front", -1)
+
+    wb12, *chunks = lax.optimization_barrier((wb12, *chunks))
+    own12 = shifted(wb12, "front", 1)
+    own12, *chunks = lax.optimization_barrier((own12, *chunks))
     all12 = lax.all_gather(own12, "helper", axis=0, tiled=True)
+    chunks[2] = shifted(chunks[2], "front", -1)
     chunks[4] = shifted(chunks[4], "front", 1)
 
     base = transposed_base(chunks, own0, all0)
     outgoing = contributions(targets, info, base, own12, all12)
     parent = place(sources, exchange(outgoing))
     diag = jnp.concatenate([diag0, diag1, diag2], axis=1)
+    factor = jnp.concatenate([factor0, factor12], axis=1)
     return factor[None], diag * diag, parent[None]
 
 

time: 345 us -> 319 us (0.925)
  waiting for transfers between devices: 162 us -> 149 us
  local copies, waits for them, and re-layouts: 19 us -> 8.67 us
  Pallas kernels: 119 us -> 112 us
    ppermute x9 -> x10, waiting for transfers between devices: 98.2 us -> 84 us  [shifted(): lax.ppermute(array, axis, [(i, (i + by) % count) for i in range(count)])]
    pallas_call x3 -> x2, Pallas kernels: 75.4 us -> 65.6 us  [factor_step(): pl.pallas_call(kernel_0 if first else kernel_12, grid=(1,), in_specs=[pl....]
    unnamed x37 -> x26, local copies, waits for them, and re-layouts: 13.9 us -> 4.19 us
    all_gather x1, waiting for transfers between devices: 0.01 us -> 4.57 us  [local(): all12 = lax.all_gather(own12, 'helper', axis=0, tiled=True)]
    all_to_all x3, waiting for transfers between devices: 63.8 us -> 60.1 us  [exchange(): lax.all_to_all(array, 'helper', split_axis=0, concat_axis=0, tiled=True)]
    ppermute x9 -> x10, starting transfers between devices: 7 us -> 10.5 us  [shifted(): lax.ppermute(array, axis, [(i, (i + by) % count) for i in range(count)])]
  transfers between devices with their start and end apart: 15 -> 16, of which waited for: 7 -> 8; matrix products, arithmetic and copies ran while one was open for 1% -> 2% of each run, Pallas kernels for 28% -> 28%
where the time goes in v3:
time: 319 us; the launch traced here: 317 us
  waiting for transfers between devices  149 us (47%)
  Pallas kernels  112 us (35%)
  starting transfers between devices  28.7 us (9%)
  between operations  14.6 us (5%)
  local copies, waits for them, and re-layouts  8.67 us (3%)
  other arithmetic  4.48 us (1%)
    ppermute x10, waiting for transfers between devices, shifted(): lax.ppermute(array, axis, [(i, (i + by) % count) for i in range(count)])  84 us
    pallas_call x2, Pallas kernels, factor_step(): pl.pallas_call(kernel_0 if first else kernel_12, grid=(1,), in_specs=[pl....  65.6 us
    all_to_all x3, waiting for transfers between devices, exchange(): lax.all_to_all(array, 'helper', split_axis=0, concat_axis=0, tiled=True)  60.1 us
    all_to_all x3, starting transfers between devices, exchange(): lax.all_to_all(array, 'helper', split_axis=0, concat_axis=0, tiled=True)  18 us
    pallas_call x1, Pallas kernels, contributions(): pl.pallas_call(contribution_kernel, grid_spec=pltpu.PrefetchScalarGridSpe...  16.2 us
    pallas_call x1, Pallas kernels, transposed_base(): pl.pallas_call(transposed_base_kernel, grid=(width // PB,), in_specs=[pl....  13 us
    ppermute x10, starting transfers between devices, shifted(): lax.ppermute(array, axis, [(i, (i + by) % count) for i in range(count)])  10.5 us
    pallas_call x1, Pallas kernels, cut(): pl.pallas_call(cut_kernel, grid=(width // PB,), in_specs=[pl.BlockSpec((1...  9.98 us
  transfers between devices with their start and end apart: 16, of which 8 were waited for; matrix products, arithmetic and copies ran while one was open for 2% of the time, Pallas kernels for 28%

profile of v3, /device:TPU:0, one launch (start us, length us, event | category | flops | bytes accessed | tf_op | source)
XLA Modules:
  0.0 317.4 jit_solution(18165907132052245784)
XLA Ops:
  7.2 1.3 dynamic-slice_bitcast_fusion.1
  8.5 1.1 pad_maximum_fusion
  9.5 8.4 %all-to-all-start = ((f32[32,8,1024]{2,1,0:T(8,128)}), f32[32,8,1024]{2,1,0:T(8,128)S(1)}, u32[]{:S(2)}, u32[]{:S(2)}) async-start(f32[32,8,1024]{2,1,0:T(8,128)} %pad_maximum_fusion), calls=%async_computation | async-start | bytes 2097152 | tf_op jit(solution)/shard_map/all_to_all | solution.py:330
  17.9 0.0 all-gather.9.cloned.1.call-start
  18.0 10.0 %cut_rows.1 = (f32[24,6656]{1,0:T(8,128)}, f32[32,6656]{1,0:T(8,128)}, f32[32,6656]{1,0:T(8,128)}, f32[80,6656]{1,0:T(8,128)}, f32[88,6656]{1,0:T(8,128)}) custom-call(f32[1,256,8192]{2,1,0:T(8,128)} %p2.1), custom_call_target="tpu_custom_call" | custom-call | tf_op jit(solution)/shard_map/cut_rows/pallas_call | solution.py:214
  28.0 7.3 %all-to-all-done = f32[32,8,1024]{2,1,0:T(8,128)S(1)} async-done(((f32[32,8,1024]{2,1,0:T(8,128)}), f32[32,8,1024]{2,1,0:T(8,128)S(1)}, u32[]{:S(2)}, u32[]{:S(2)}) %all-to-all-start) | async-done | bytes 1048608 | tf_op jit(solution)/shard_map/all_to_all | solution.py:330
  35.3 0.7 slice.16
  36.0 0.0 all-gather.9.cloned.1.call-update
  36.0 0.8 slice.13
  36.8 1.1 broadcast_in_dim.31
  37.9 3.9 %all-to-all-start.1 = ((f32[32,2,8,512]{3,2,1,0:T(8,128)}), f32[32,2,8,512]{3,2,1,0:T(8,128)S(1)}, u32[]{:S(2)}, u32[]{:S(2)}) async-start(f32[32,2,8,512]{3,2,1,0:T(8,128)} %broadcast_in_dim.31), calls=%async_computation.1 | async-start | bytes 2097152 | tf_op jit(solution)/shard_map/all_to_all | solution.py:330
  41.8 0.0 all-gather.5.cloned.1.call-start
  41.8 1.6 collective-permute-start
  43.4 16.4 %collective-permute-done.refs_0_ = f32[24,6656]{1,0:T(8,128)S(1)} collective-permute-done((f32[24,6656]{1,0:T(8,128)}, f32[24,6656]{1,0:T(8,128)S(1)}, u32[]{:S(2)}, u32[]{:S(2)}) %collective-permute-start) | collective-permute-done | bytes 639008 | tf_op jit(solution)/shard_map/ppermute | solution.py:25
  59.8 2.0 all-to-all-done.1.a00
  61.8 1.4 collective-permute-start.1
  63.3 1.8 collective-permute-start.2
  65.1 18.6 %pivot_block_0.1 = (f32[512,512]{1,0:T(8,128)S(1)}, f32[1,512]{1,0:T(1,128)S(1)}, f32[256,512]{1,0:T(8,128)S(1)}, bf16[256,512]{1,0:T(8,128)(2,1)S(1)}) custom-call(s32[1]{0:T(128)} %bitcast.row_ref, f32[32,2,8,512]{3,2,1,0:T(8,128)S(1)} %all-to-all-done.1.a00, f32[1,256,8192]{2,1,0:T(8,128)} %p2.1), custom_call_target="tpu_custom_call" | custom-call | flops 20000000000 | bytes 4000000 | tf_op jit(solution)/shard_map/pivot_block_0/pallas_call | solution.py:191
  83.7 0.0 copy-start.4
  83.7 0.8 copy-done.4
  84.5 1.0 copy-done.7
  85.4 0.0 collective-permute-done.1.refs_1_
  85.4 0.0 collective-permute-done.2
  85.4 0.0 copy-start.11
  85.4 0.9 copy-done.11
  86.4 0.2 collective-permute-start.3
  86.6 8.1 %collective-permute-done.3.own = bf16[256,512]{1,0:T(8,128)(2,1)S(1)} collective-permute-done((bf16[256,512]{1,0:T(8,128)(2,1)S(1)}, bf16[256,512]{1,0:T(8,128)(2,1)S(1)}, u32[]{:S(2)}, u32[]{:S(2)}) %collective-permute-start.3) | collective-permute-done | bytes 262176 | tf_op jit(solution)/shard_map/ppermute | solution.py:25
  94.7 0.7 copy-done.2
  95.4 0.0 all-gather.5.cloned.1.call-update
  95.4 0.0 all-gather.7.cloned.1.call-start
  95.5 0.4 collective-permute-start.5
  95.9 1.7 collective-permute-start.6
  97.6 0.0 copy-done.6
  97.6 47.0 %pivot_block_1.1 = (f32[1,512]{1,0:T(1,128)}, f32[1,512]{1,0:T(1,128)}, f32[256,1024]{1,0:T(8,128)}, bf16[256,1024]{1,0:T(8,128)(2,1)}) custom-call(s32[1]{0:T(128)} %bitcast.row_ref, f32[32,6,8,1024]{3,2,1,0:T(8,128)} %bitcast.15, f32[32,6,8,1024]{3,2,1,0:T(8,128)} %bitcast.16, f32[32,6,8,1024]{3,2,1,0:T(8,128)} %bitcast.17, f32[32,6,8,1024]{3,2,1,0:T(8,128)} %bitcast.18, ...), custom_call_target="tpu_custom_call" | custom-call | flops 40000000000 | bytes 4000000 | tf_op jit(solution)/shard_map/pivot_block_1/pallas_call | solution.py:191
  144.6 0.0 collective-permute-done.5
  144.6 0.0 collective-permute-done.6.refs_3_
  144.6 0.1 collective-permute-start.7
  144.7 12.7 %collective-permute-done.7.own = bf16[256,1024]{1,0:T(8,128)(2,1)S(1)} collective-permute-done((bf16[256,1024]{1,0:T(8,128)(2,1)}, bf16[256,1024]{1,0:T(8,128)(2,1)S(1)}, u32[]{:S(2)}, u32[]{:S(2)}) %collective-permute-start.7) | collective-permute-done | bytes 524320 | tf_op jit(solution)/shard_map/ppermute | solution.py:25
  157.4 0.8 copy-done
  158.2 0.0 all-gather.7.cloned.1.call-update
  158.2 0.1 collective-permute-start.9
  158.3 3.2 %collective-permute-start.8 = (f32[32,6656]{1,0:T(8,128)}, f32[32,6656]{1,0:T(8,128)S(1)}, u32[]{:S(2)}, u32[]{:S(2)}) collective-permute-start(f32[32,6656]{1,0:T(8,128)} %collective-permute-done.5), channel_id=1, source_target_pairs={{0,96},{32,0},{64,32},{96,64},{1,97},{33,1},{65,33},{97,65},{2,98}... | collective-permute-start | bytes 2555912 | tf_op jit(solution)/shard_map/ppermute | solution.py:25
  162.2 0.0 copy-done.12
  162.2 0.1 pad_add_fusion
  162.2 0.0 collective-permute-start.4
  162.3 46.9 %collective-permute-done.4 = s32[53]{0:T(128)S(1)} collective-permute-done((s32[53]{0:T(128)S(1)}, s32[53]{0:T(128)S(1)}, u32[]{:S(2)}, u32[]{:S(2)}) %collective-permute-start.4) | collective-permute-done | bytes 244 | tf_op jit(solution)/shard_map/ppermute | solution.py:25
  209.1 0.6 slice.15
  209.8 0.7 pad_add_fusion.1.info_ref
  210.5 0.0 collective-permute-done.8.refs_2_
  210.5 0.0 collective-permute-done.9.refs_4_
  210.5 0.0 all-gather.5.cloned.1.call-done.w
  210.5 0.0 copy-done.3
  210.5 13.0 %transposed_base.1.base = f32[6656,256]{1,0:T(8,128)} custom-call(bf16[8192,512]{1,0:T(8,128)(2,1)} %all-gather.5.cloned.1.call-done.w, bf16[256,512]{1,0:T(8,128)(2,1)S(1)} %copy-done.3, f32[24,6656]{1,0:T(8,128)S(1)} %collective-permute-done.refs_0_, f32[32,6656]{1,0:T(8,128)S(1)} %collective-permute-done.1.refs_1_, ...), custom_call_target="tpu_custom_call" | custom-call | tf_op jit(solution)/shard_map/transposed_base/pallas_call | solution.py:239
  223.5 4.6 %all-gather.7.cloned.1.call-done.w = bf16[8192,1024]{1,0:T(8,128)(2,1)} async-done(((bf16[256,1024]{1,0:T(8,128)(2,1)}), bf16[8192,1024]{1,0:T(8,128)(2,1)}) %all-gather.7.cloned.1.call-update) | async-done | bytes 16777232 | tf_op jit(solution)/shard_map/all_gather | solution.py:382
  228.1 0.0 copy-done.1
  228.1 16.2 %contributions.1 = bf16[32,256,256]{2,1,0:T(8,128)(2,1)} custom-call(s32[52]{0:T(128)S(1)} %bitcast.12, s32[2]{0:T(128)S(1)} %pad_add_fusion.1.info_ref, f32[6656,256]{1,0:T(8,128)} %transposed_base.1.base, bf16[8192,1024]{1,0:T(8,128)(2,1)} %all-gather.7.cloned.1.call-done.w, bf16[256,1024]{1,0:T(8,128)(2,1)S(1)} %copy-done.1), custom_call_target="tpu_custom_call" | custom-call | tf_op jit(solution)/shard_map/contributions/pallas_call | solution.py:276
  244.2 0.0 copy-start.8
  244.2 5.7 %all-to-all-start.2 = ((bf16[32,256,256]{2,1,0:T(8,128)(2,1)}), bf16[32,256,256]{2,1,0:T(8,128)(2,1)}, u32[]{:S(2)}, u32[]{:S(2)}) async-start(bf16[32,256,256]{2,1,0:T(8,128)(2,1)} %contributions.1), calls=%async_computation.2 | async-start | bytes 8388608 | tf_op jit(solution)/shard_map/all_to_all | solution.py:330
  249.9 0.6 iota_compare_fusion.1
  250.6 0.1 select_reduce_fusion
  250.7 0.6 maximum_multiply_fusion
  251.3 1.3 maximum_bitcast_fusion
  252.6 50.8 %all-to-all-done.2.refs_0_.refs_1_.refs_2_.refs_3_.refs_4_.refs_5_.refs_6_.refs_7_ = bf16[32,256,256]{2,1,0:T(8,128)(2,1)} async-done(((bf16[32,256,256]{2,1,0:T(8,128)(2,1)}), bf16[32,256,256]{2,1,0:T(8,128)(2,1)}, u32[]{:S(2)}, u32[]{:S(2)}) %all-to-all-start.2) | async-done | bytes 4194336 | tf_op jit(solution)/shard_map/all_to_all | solution.py:330
  303.4 7.5 %parent_rows.1 = bf16[256,8192]{1,0:T(8,128)(2,1)} custom-call(s32[64]{0:T(128)S(1)} %compare_select_fusion.source_ref, bf16[32,256,256]{2,1,0:T(8,128)(2,1)} %all-to-all-done.2.refs_0_.refs_1_.refs_2_.refs_3_.refs_4_.refs_5_.refs_6_.refs_7_, bf16[32,256,256]{2,1,0:T(8,128)(2,1)} %all-to-all-done.2.refs_0_.refs_1_.refs_2_.refs_3_.refs_4_.refs_5_.refs_6_.refs_7_, ...), custom_call_target="tpu_custom_call" | custom-call | tf_op jit(solution)/shard_map/parent_rows/pallas_call | solution.py:315
  (17 shorter events, 0.0 us)
Async XLA Ops:
  9.5 25.8 %all-to-all-start = ((f32[32,8,1024]{2,1,0:T(8,128)}), f32[32,8,1024]{2,1,0:T(8,128)S(1)}, u32[]{:S(2)}, u32[]{:S(2)}) async-start(f32[32,8,1024]{2,1,0:T(8,128)} %pad_maximum_fusion), calls=%async_computation | async-start | bytes 2097152 | tf_op jit(solution)/shard_map/all_to_all | solution.py:330
  17.9 79.6 %all-gather.9.cloned.1.call-start = ((), (), s32[]{:S(2)}) async-start(), calls=%async_computation.5 | async-start | bytes 6488064 | tf_op jit(solution)/shard_map/all_gather | solution.py:349
  37.9 24.0 %all-to-all-start.1 = ((f32[32,2,8,512]{3,2,1,0:T(8,128)}), f32[32,2,8,512]{3,2,1,0:T(8,128)S(1)}, u32[]{:S(2)}, u32[]{:S(2)}) async-start(f32[32,2,8,512]{3,2,1,0:T(8,128)} %broadcast_in_dim.31), calls=%async_computation.1 | async-start | bytes 2097152 | tf_op jit(solution)/shard_map/all_to_all | solution.py:330
  41.8 168.7 %all-gather.5.cloned.1.call-start = ((), (), s32[]{:S(2)}) async-start(), calls=%async_computation.3 | async-start | bytes 8650752 | tf_op jit(solution)/shard_map/all_gather | solution.py:367
  41.8 17.9 %collective-permute-start = (f32[24,6656]{1,0:T(8,128)}, f32[24,6656]{1,0:T(8,128)S(1)}, u32[]{:S(2)}, u32[]{:S(2)}) collective-permute-start(f32[24,6656]{1,0:T(8,128)} %get-tuple-element.59), channel_id=1, source_target_pairs={{0,32},{32,64},{64,96},{96,0},{1,33},{33,65},{65,97},{97,1},{2,34}... | collective-permute-start | bytes 1916936 | tf_op jit(solution)/shard_map/ppermute | solution.py:25
  61.8 23.6 %collective-permute-start.1 = (f32[32,6656]{1,0:T(8,128)}, f32[32,6656]{1,0:T(8,128)S(1)}, u32[]{:S(2)}, u32[]{:S(2)}) collective-permute-start(f32[32,6656]{1,0:T(8,128)} %get-tuple-element.69), channel_id=1, source_target_pairs={{0,32},{32,64},{64,96},{96,0},{1,33},{33,65},{65,97},{97,1},{2,34}... | collective-permute-start | bytes 2555912 | tf_op jit(solution)/shard_map/ppermute | solution.py:25
  63.3 22.2 %collective-permute-start.2 = (f32[32,6656]{1,0:T(8,128)}, f32[32,6656]{1,0:T(8,128)S(1)}, u32[]{:S(2)}, u32[]{:S(2)}) collective-permute-start(f32[32,6656]{1,0:T(8,128)} %get-tuple-element.70), channel_id=1, source_target_pairs={{0,96},{32,0},{64,32},{96,64},{1,97},{33,1},{65,33},{97,65},{2,98}... | collective-permute-start | bytes 2555912 | tf_op jit(solution)/shard_map/ppermute | solution.py:25
  83.7 0.8 copy-start.4
  84.5 1.0 copy-start.7
  85.4 12.2 %copy-start.6 = (bf16[256,512]{1,0:T(8,128)(2,1)}, bf16[256,512]{1,0:T(8,128)(2,1)S(1)}, u32[]{:S(2)}) copy-start(bf16[256,512]{1,0:T(8,128)(2,1)S(1)} %get-tuple-element.73.wb0) | copy-start | bytes 786436
  85.4 0.9 copy-start.11
  86.4 8.3 %collective-permute-start.3 = (bf16[256,512]{1,0:T(8,128)(2,1)S(1)}, bf16[256,512]{1,0:T(8,128)(2,1)S(1)}, u32[]{:S(2)}, u32[]{:S(2)}) collective-permute-start(bf16[256,512]{1,0:T(8,128)(2,1)S(1)} %get-tuple-element.73.wb0), channel_id=1, source_target_pairs={{0,32},{32,64},{64,96},{96,0},{1,33},{33,65},{65,97},{97,1},{2,34}... | collective-permute-start | bytes 786440 | tf_op jit(solution)/shard_map/ppermute | solution.py:25
  94.7 0.7 copy-start.2
  95.4 132.6 %all-gather.7.cloned.1.call-start = ((), (), s32[]{:S(2)}) async-start(), calls=%async_computation.4 | async-start | bytes 17301504 | tf_op jit(solution)/shard_map/all_gather | solution.py:382
  95.5 49.1 %collective-permute-start.5 = (f32[32,6656]{1,0:T(8,128)}, f32[32,6656]{1,0:T(8,128)}, u32[]{:S(2)}, u32[]{:S(2)}) collective-permute-start(f32[32,6656]{1,0:T(8,128)} %copy-done.11), channel_id=1, source_target_pairs={{0,96},{32,0},{64,32},{96,64},{1,97},{33,1},{65,33},{97,65},{2,98}... | collective-permute-start | bytes 2555912 | tf_op jit(solution)/shard_map/ppermute | solution.py:25
  95.9 48.7 %collective-permute-start.6 = (f32[80,6656]{1,0:T(8,128)}, f32[80,6656]{1,0:T(8,128)}, u32[]{:S(2)}, u32[]{:S(2)}) collective-permute-start(f32[80,6656]{1,0:T(8,128)} %get-tuple-element.89), channel_id=1, source_target_pairs={{0,32},{32,64},{64,96},{96,0},{1,33},{33,65},{65,97},{97,1},{2,34}... | collective-permute-start | bytes 6389768 | tf_op jit(solution)/shard_map/ppermute | solution.py:25
  97.6 64.6 %copy-start.12 = (s32[1,52]{1,0:T(1,128)S(1)}, s32[1,52]{1,0:T(1,128)}, u32[]{:S(2)}) copy-start(s32[1,52]{1,0:T(1,128)} %param.4) | copy-start | bytes 628
  97.6 113.0 %copy-start.3 = (bf16[256,512]{1,0:T(8,128)(2,1)S(1)}, bf16[256,512]{1,0:T(8,128)(2,1)}, u32[]{:S(2)}) copy-start(bf16[256,512]{1,0:T(8,128)(2,1)} %copy-done.2) | copy-start | bytes 786436
  144.6 12.8 %collective-permute-start.7 = (bf16[256,1024]{1,0:T(8,128)(2,1)}, bf16[256,1024]{1,0:T(8,128)(2,1)S(1)}, u32[]{:S(2)}, u32[]{:S(2)}) collective-permute-start(bf16[256,1024]{1,0:T(8,128)(2,1)} %get-tuple-element.91), channel_id=1, source_target_pairs={{0,32},{32,64},{64,96},{96,0},{1,33},{33,65},{65,97},{97,1},{2,34}... | collective-permute-start | bytes 1572872 | tf_op jit(solution)/shard_map/ppermute | solution.py:25
  157.4 0.8 copy-start
  158.2 52.3 %collective-permute-start.9 = (f32[88,6656]{1,0:T(8,128)}, f32[88,6656]{1,0:T(8,128)}, u32[]{:S(2)}, u32[]{:S(2)}) collective-permute-start(f32[88,6656]{1,0:T(8,128)} %get-tuple-element.101), channel_id=1, source_target_pairs={{0,32},{32,64},{64,96},{96,0},{1,33},{33,65},{65,97},{97,1},{2,34}... | collective-permute-start | bytes 7028744 | tf_op jit(solution)/shard_map/ppermute | solution.py:25
  158.3 52.2 %collective-permute-start.8 = (f32[32,6656]{1,0:T(8,128)}, f32[32,6656]{1,0:T(8,128)S(1)}, u32[]{:S(2)}, u32[]{:S(2)}) collective-permute-start(f32[32,6656]{1,0:T(8,128)} %collective-permute-done.5), channel_id=1, source_target_pairs={{0,96},{32,0},{64,32},{96,64},{1,97},{33,1},{65,33},{97,65},{2,98}... | collective-permute-start | bytes 2555912 | tf_op jit(solution)/shard_map/ppermute | solution.py:25
  162.2 46.9 %collective-permute-start.4 = (s32[53]{0:T(128)S(1)}, s32[53]{0:T(128)S(1)}, u32[]{:S(2)}, u32[]{:S(2)}) collective-permute-start(s32[53]{0:T(128)S(1)} %pad_add_fusion), channel_id=1, source_target_pairs={{0,32},{32,64},{64,96},{96,0},{1,33},{33,65},{65,97},{97,1},{2,34}... | collective-permute-start | bytes 644 | tf_op jit(solution)/shard_map/ppermute | solution.py:25
  210.5 17.6 %copy-start.1 = (bf16[256,1024]{1,0:T(8,128)(2,1)S(1)}, bf16[256,1024]{1,0:T(8,128)(2,1)}, u32[]{:S(2)}) copy-start(bf16[256,1024]{1,0:T(8,128)(2,1)} %copy-done) | copy-start | bytes 1572868
  244.2 6.5 %copy-start.9 = (f32[1,512]{1,0:T(1,128)S(1)}, f32[1,512]{1,0:T(1,128)}, u32[]{:S(2)}) copy-start(f32[1,512]{1,0:T(1,128)} %get-tuple-element.82) | copy-start | bytes 6148
  244.2 6.5 %copy-start.10 = (f32[1,512]{1,0:T(1,128)S(1)}, f32[1,512]{1,0:T(1,128)}, u32[]{:S(2)}) copy-start(f32[1,512]{1,0:T(1,128)} %get-tuple-element.83) | copy-start | bytes 6148
  244.2 7.1 %copy-start.5 = (f32[256,512]{1,0:T(8,128)S(1)}, f32[256,512]{1,0:T(8,128)}, u32[]{:S(2)}) copy-start(f32[256,512]{1,0:T(8,128)} %copy-done.4) | copy-start | bytes 1572868
  244.2 7.1 %copy-start.8 = (f32[256,1024]{1,0:T(8,128)S(1)}, f32[256,1024]{1,0:T(8,128)}, u32[]{:S(2)}) copy-start(f32[256,1024]{1,0:T(8,128)} %get-tuple-element.80) | copy-start | bytes 3145732
  244.2 59.2 %all-to-all-start.2 = ((bf16[32,256,256]{2,1,0:T(8,128)(2,1)}), bf16[32,256,256]{2,1,0:T(8,128)(2,1)}, u32[]{:S(2)}, u32[]{:S(2)}) async-start(bf16[32,256,256]{2,1,0:T(8,128)(2,1)} %contributions.1), calls=%async_computation.2 | async-start | bytes 8388608 | tf_op jit(solution)/shard_map/all_to_all | solution.py:330
Sparse Core Ops, SparseCore 0:
  36.1 53.3 all-gather.8
  95.5 49.8 all-gather.4
  158.3 69.6 all-gather.6
